TPU v7x, 512 devices: a whole 4x8x8 slice. The times are simulated.
512 devices in a mesh: rows: 256 (over x, z, y), feat: 2 (over core).
Axes of the slice: x: 4, y: 8, z: 8, core: 2. Of those that a mesh axis runs over, the one named last changes fastest.
Arguments:
- embeddings: bfloat16 [196608, 768], P('rows', 'feat'), may hold values from -6 to 6
- factor: float32 [196608, 256], P(('rows', 'feat')), may hold values from -0.1 to 0.1, as said below
- residual_diag: float32 [196608], P(('rows', 'feat')), may hold values from 0.5 to 1.5
- pivots: int32 [2, 256], replicated, may hold values from 0 to 196607, as said below
Outputs:
- new_columns: float32 [2, 196608, 256], P(None, ('rows', 'feat'))
- residual_out: float32 [196608], P(('rows', 'feat'))
Inputs may be any that keep to these rules, and one draw needn't show every extreme that they name: Each block's 256 pivots are distinct and increasing, the two blocks share none, and in each block at most 2 pivots lie among the 768 candidates of one index of rows; some index holds exactly 2 in every block. `factor`: entries are independent.
All inputs are finite; a program needn't handle non-finite values.
Results may differ from a plain program's by a relative error of at most 0.0003.
Values may be sent and summed in bfloat16 or wider, within the bound.
A program may use at most 64 MiB of HBM per device.

v0:
```python
import jax
import jax.numpy as jnp
from jax import lax
from jax.sharding import PartitionSpec as P

ridge_weight = 2.0


def shards(embeddings, factor, residual_diag, pivots):
    local_rows = embeddings.shape[0]
    half_rows = factor.shape[0]
    feat_cols = embeddings.shape[1]
    feat_count = lax.axis_size("feat")
    full_width = feat_cols * feat_count
    row_group = lax.axis_index("rows")
    feat_group = lax.axis_index("feat")
    rows_start = row_group * local_rows
    half_start = rows_start + feat_group * half_rows
    global_ids = half_start + jnp.arange(half_rows, dtype=jnp.int32)
    partial_norms = jnp.sum(jnp.square(embeddings.astype(jnp.float32)), axis=1)
    row_norms = partial_norms
    current = factor
    fresh_list = []
    for block_id in range(2):
        chosen_ids = pivots[block_id]
        pivot_count = chosen_ids.shape[0]
        offsets = chosen_ids - rows_start
        owned_mask = (offsets >= 0) & (offsets < local_rows)
        safe_rows = jnp.clip(offsets, 0, local_rows - 1)
        half_offsets = offsets - feat_group * half_rows
        half_mask = owned_mask & (half_offsets >= 0) & (half_offsets < half_rows)
        half_safe = jnp.clip(half_offsets, 0, half_rows - 1)
        own_rows = jnp.where(
            owned_mask[:, None], jnp.take(embeddings, safe_rows, axis=0).astype(jnp.float32), 0.0
        )
        spread = jnp.zeros((pivot_count, full_width), jnp.float32)
        spread = lax.dynamic_update_slice_in_dim(spread, own_rows, feat_group * feat_cols, 1)
        own_factor = jnp.where(half_mask[:, None], jnp.take(current, half_safe, axis=0), 0.0)
        summed_rows = lax.psum(spread, ("rows", "feat"))
        pivot_factor = lax.psum(own_factor, ("rows", "feat"))
        chosen = summed_rows.astype(jnp.bfloat16)
        own_cols = lax.dynamic_slice_in_dim(chosen, feat_group * feat_cols, feat_cols, 1)
        dots_part = jnp.einsum(
            "nd,kd->nk", embeddings, own_cols, preferred_element_type=jnp.float32
        )
        partial_terms = (dots_part, partial_norms) if block_id == 0 else (dots_part,)
        summed = lax.psum_scatter(partial_terms, "feat", scatter_dimension=0, tiled=True)
        dot_panel = summed[0]
        if block_id == 0:
            row_norms = summed[1]
        chosen_wide = chosen.astype(jnp.float32)
        chosen_norms = jnp.sum(chosen_wide * chosen_wide, axis=1)
        kernel_panel = jnp.exp(
            -(row_norms[:, None] + chosen_norms[None, :] - 2.0 * dot_panel) / (2.0 * full_width)
        )
        kernel_panel = kernel_panel + ridge_weight * (
            global_ids[:, None] == chosen_ids[None, :]
        ).astype(jnp.float32)
        kernel_panel = kernel_panel - jnp.dot(
            current,
            pivot_factor.T,
            precision=lax.Precision.HIGHEST,
            preferred_element_type=jnp.float32,
        )
        pivot_dots = jnp.einsum("kd,jd->kj", chosen, chosen, preferred_element_type=jnp.float32)
        pivot_block = jnp.exp(
            -(chosen_norms[:, None] + chosen_norms[None, :] - 2.0 * pivot_dots) / (2.0 * full_width)
        )
        pivot_block = pivot_block + ridge_weight * jnp.eye(pivot_count, dtype=jnp.float32)
        pivot_block = pivot_block - jnp.dot(
            pivot_factor,
            pivot_factor.T,
            precision=lax.Precision.HIGHEST,
            preferred_element_type=jnp.float32,
        )
        chol_lower = jnp.linalg.cholesky(pivot_block)
        fresh_cols = jax.scipy.linalg.solve_triangular(chol_lower, kernel_panel.T, lower=True).T
        fresh_list.append(fresh_cols)
        current = jnp.concatenate([current, fresh_cols], axis=1)
    removed = jnp.sum(fresh_list[0] * fresh_list[0], axis=1) + jnp.sum(
        fresh_list[1] * fresh_list[1], axis=1
    )
    return (jnp.stack(fresh_list), residual_diag - removed)


def solution(mesh):
    return jax.shard_map(
        shards,
        mesh=mesh,
        in_specs=(P("rows", "feat"), P(("rows", "feat"), None), P(("rows", "feat")), P()),
        out_specs=(P(None, ("rows", "feat"), None), P(("rows", "feat"))),
        check_vma=False,
    )
```

profile of v0, /device:TPU:1, one launch (start us, length us, event | category | flops | bytes accessed | tf_op | source)
XLA Modules:
  0.0 698.0 jit_solution(3108703328044418488)
XLA Ops:
  9.6 2.0 gather_fusion
  15.4 114.3 %all-reduce.10 = (bf16[256,768]{1,0:T(8,128)(2,1)S(1)}, bf16[256,768]{1,0:T(8,128)(2,1)}) all-reduce(f32[256,768]{1,0:T(8,128)S(1)} %select_dynamic-update-slice_fusion.1, f32[256,768]{1,0:T(8,128)S(1)} %select_dynamic-update-slice_fusion), channel_id=1, replica_groups=mesh['rows'=256,'feat'=2] {'rows','feat'}, use_global_device_ids=true, to_apply=%region_0.2 | all-reduce | flops 393216 | bytes 2359296 | tf_op jit(solution)/shard_map/psum | solution.py:39
  132.5 2.6 all-reduce.1
  135.1 1.3 dynamic-slice.5
  137.2 150.0 %all-reduce.7.cloned.1.call-done = f32[256,256]{0,1:T(8,128)} async-done(((f32[256,256]{0,1:T(8,128)}), f32[256,256]{0,1:T(8,128)}) %all-reduce.7.cloned.1.call-update) | async-done | bytes 262160 | tf_op jit(solution)/shard_map/psum | solution.py:40
  287.2 1.6 convolution_subtract_fusion.1
  289.0 11.7 %cholesky.130 = f32[128,128]{1,0:T(8,128)S(1)} custom-call(f32[128,128]{1,0:T(8,128)S(1)} %cholesky.194), custom_call_target="Cholesky" | custom-call | tf_op jit(solution)/shard_map/jit(cholesky)/cholesky | solution.py:76
  300.8 9.8 %custom-call.13 = f32[1,128,128]{1,2,0:T(8,128)S(1)} custom-call(f32[1,128,128]{2,1,0:T(8,128)S(1)} %get-tuple-element.62), custom_call_target="InvertDiagBlocksLowerTriangular" | custom-call | tf_op jit(solution)/shard_map/jit(cholesky)/cholesky | solution.py:76
  311.1 11.7 %cholesky.147 = f32[128,128]{1,0:T(8,128)S(1)} custom-call(f32[128,128]{1,0:T(8,128)S(1)} %convolution_subtract_fusion.6), custom_call_target="Cholesky" | custom-call | tf_op jit(solution)/shard_map/jit(cholesky)/cholesky | solution.py:76
  325.7 4.3 while.4
  326.6 1.4 bitcast_dynamic-update-slice_fusion.4
  328.6 1.4 bitcast_dynamic-update-slice_fusion.4
  330.0 19.7 %custom-call.14 = f32[2,128,128]{1,2,0:T(8,128)S(1)} custom-call(f32[2,128,128]{2,1,0:T(8,128)S(1)} %get-tuple-element.19), custom_call_target="InvertDiagBlocksLowerTriangular" | custom-call | tf_op jit(solution)/shard_map/jit(_solve_triangular)/triangular_solve | solution.py:77
  349.8 2.0 fusion.2
  357.9 264.1 %all-reduce.9.cloned.1.call-done = f32[256,512]{1,0:T(8,128)} async-done(((f32[256,512]{1,0:T(8,128)}), f32[256,512]{1,0:T(8,128)}) %all-reduce.9.cloned.1.call-update) | async-done | bytes 524304 | tf_op jit(solution)/shard_map/psum | solution.py:40
  622.0 1.8 convolution_subtract_fusion.2
  624.0 11.7 %cholesky.164 = f32[128,128]{1,0:T(8,128)S(1)} custom-call(f32[128,128]{1,0:T(8,128)S(1)} %cholesky.197), custom_call_target="Cholesky" | custom-call | tf_op jit(solution)/shard_map/jit(cholesky)/cholesky | solution.py:76
  635.8 9.8 %custom-call.15 = f32[1,128,128]{1,2,0:T(8,128)S(1)} custom-call(f32[1,128,128]{2,1,0:T(8,128)S(1)} %get-tuple-element.58), custom_call_target="InvertDiagBlocksLowerTriangular" | custom-call | tf_op jit(solution)/shard_map/jit(cholesky)/cholesky | solution.py:76
  646.1 11.7 %cholesky.181 = f32[128,128]{1,0:T(8,128)S(1)} custom-call(f32[128,128]{1,0:T(8,128)S(1)} %convolution_subtract_fusion.5), custom_call_target="Cholesky" | custom-call | tf_op jit(solution)/shard_map/jit(cholesky)/cholesky | solution.py:76
  660.5 4.3 while.5
  661.5 1.3 bitcast_dynamic-update-slice_fusion.5
  663.5 1.3 bitcast_dynamic-update-slice_fusion.5
  664.9 19.7 %custom-call.16 = f32[2,128,128]{1,2,0:T(8,128)S(1)} custom-call(f32[2,128,128]{2,1,0:T(8,128)S(1)} %get-tuple-element.20), custom_call_target="InvertDiagBlocksLowerTriangular" | custom-call | tf_op jit(solution)/shard_map/jit(_solve_triangular)/triangular_solve | solution.py:77
  684.6 2.0 fusion
  (100 shorter events, 24.7 us)
Async XLA Ops:
  8.0 279.2 %all-reduce.7.cloned.1.call-start = ((), (), s32[]{:S(2)}) async-start(), calls=%async_computation.2 | async-start | bytes 524288 | tf_op jit(solution)/shard_map/psum | solution.py:40
  11.6 1.1 copy-start
  12.5 337.3 %reduce-scatter.3.cloned.1.call-start = ((), (), s32[]{:S(2)}) async-start(), calls=%async_computation.3 | async-start | bytes 1179648 | tf_op jit(solution)/shard_map/reduce_scatter | solution.py:47
  131.0 1.0 copy-start.1
  131.0 491.0 %all-reduce.9.cloned.1.call-start = ((), (), s32[]{:S(2)}) async-start(), calls=%async_computation.4 | async-start | bytes 1048576 | tf_op jit(solution)/shard_map/psum | solution.py:40
  322.8 26.9 %copy-start.3 = (f32[256,256]{0,1:T(8,128)S(1)}, f32[256,256]{0,1:T(8,128)}, u32[]{:S(2)}) copy-start(f32[256,256]{0,1:T(8,128)} %all-reduce.7.cloned.1.call-done) | copy-start | bytes 786436
  355.0 1.0 copy-start.5
  356.0 328.6 %reduce-scatter.5.cloned.1.call-start = ((), (), s32[]{:S(2)}) async-start(), calls=%async_computation.5 | async-start | bytes 1179648 | tf_op jit(solution)/shard_map/reduce_scatter | solution.py:47
  657.8 26.8 %copy-start.2 = (f32[256,512]{1,0:T(8,128)S(1)}, f32[256,512]{1,0:T(8,128)}, u32[]{:S(2)}) copy-start(f32[256,512]{1,0:T(8,128)} %all-reduce.9.cloned.1.call-done) | copy-start | bytes 1572868
  687.4 1.0 copy-start.4
  688.4 1.2 copy-start.6
Sparse Core Ops, SparseCore 0:
  13.8 273.3 all-reduce.6
  356.1 265.8 all-reduce.8
Sparse Core Ops, SparseCore 1:
  131.1 11.1 reduce-scatter.2
  360.1 14.0 reduce-scatter.4
where the time goes:
time: 708 us; the launch traced here: 698 us
  waiting for transfers between devices  414 us (58%)
  blocking collectives  117 us (17%)
  other arithmetic  114 us (16%)
  between operations  19.7 us (3%)
  local copies, waits for them, and re-layouts  18.9 us (3%)
  matrix products  13.8 us (2%)
    psum x2, waiting for transfers between devices, shards(): pivot_factor = lax.psum(own_factor, ('rows', 'feat'))  414 us
    psum x1, blocking collectives, shards(): summed_rows = lax.psum(spread, ('rows', 'feat'))  114 us
    another operation x14, other arithmetic, shards(): chol_lower = jnp.linalg.cholesky(pivot_block)  69.3 us
    another operation x5, other arithmetic, shards(): jax.scipy.linalg.solve_triangular(chol_lower, kernel_panel.T, lower=True)  39.4 us
  transfers between devices with their start and end apart: 4, of which 2 were waited for; matrix products, arithmetic and copies ran while one was open for 19% of the time, Pallas kernels for 0%

commit v1 on v0

v1 whole, which is shorter than its diff:
```python
import functools

import jax
import jax.numpy as jnp
from jax import lax
from jax.experimental import pallas as pl
from jax.experimental.pallas import tpu as pltpu
from jax.sharding import PartitionSpec as P

F32 = jnp.float32
BF16 = jnp.bfloat16
ridge_weight = 2.0
TILE = 128
SUB = 8


def dot(a, b, dims):
    return lax.dot_general(a, b, (dims, ((), ())), preferred_element_type=F32)


NN = ((1,), (0,))
NT = ((1,), (1,))
TN = ((0,), (0,))


def split2(x):
    hi = x.astype(BF16)
    return hi, (x - hi.astype(F32)).astype(BF16)


def dot3(a, b, dims):
    return dot(a[0], b[0], dims) + (dot(a[0], b[1], dims) + dot(a[1], b[0], dims))


def norm_lanes(rows, first):
    wide = rows.astype(F32)
    neg = jnp.sum(wide * wide, axis=1, keepdims=True) * -0.5
    hi = neg.astype(BF16).astype(F32)
    mid = (neg - hi).astype(BF16).astype(F32)
    low = (neg - hi) - mid
    lane = lax.broadcasted_iota(jnp.int32, (rows.shape[0], TILE), 1)
    at = 0 if first else 3
    out = jnp.where(lane < 6, 1.0, 0.0)
    out = jnp.where(lane == at, hi, out)
    out = jnp.where(lane == at + 1, mid, out)
    out = jnp.where(lane == at + 2, low, out)
    return out.astype(BF16)


def factor_tile(s_ref, cb_ref, pb_ref):
    count = TILE // SUB
    shape = (SUB, TILE)
    lane = lax.broadcasted_iota(jnp.int32, shape, 1)

    def rows(i):
        return s_ref[SUB * i : SUB * (i + 1), :]

    def lane_copy(x, at):
        return jnp.broadcast_to(x[:, at : at + 1], shape)

    def row_copy(ref, at):
        return jnp.broadcast_to(ref[at : at + 1, :], shape)

    ahead = [lane_copy(rows(0), j) for j in range(SUB)]
    for k in range(count):
        base = SUB * k
        diag = (lane >= base) & (lane < base + SUB)
        for j in range(SUB):
            cb_ref[SUB * j : SUB * (j + 1), :] = ahead[j]
        a = [[row_copy(cb_ref, SUB * q + m) if q <= m else None for q in range(SUB)] for m in range(SUB)]
        raw = {}
        for i in range(k + 1, count):
            block = rows(i)
            raw[i] = [lane_copy(block, base + j) for j in range(SUB)]
        near = {i: list(raw[i]) for i in range(k + 1, min(k + 3, count))}
        r = [jnp.where(diag, jnp.where(lane == base + j, 1.0, 0.0), row_copy(s_ref, base + j)) for j in range(SUB)]
        if k + 1 < count:
            block = rows(k + 1)
            ahead = [lane_copy(block, base + SUB + j) for j in range(SUB)]
        inv = []
        low = [[None] * SUB for _ in range(SUB)]
        for j in range(SUB):
            inv.append(lax.rsqrt(a[j][j]))
            for m in range(j + 1, SUB):
                low[m][j] = a[m][j] * inv[j]
            for q in range(j + 1, SUB):
                for m in range(q, SUB):
                    a[m][q] = a[m][q] - low[m][j] * low[q][j]
            for i in near:
                near[i][j] = near[i][j] * inv[j]
                for m in range(j + 1, SUB):
                    near[i][m] = near[i][m] - near[i][j] * low[m][j]
            if k + 1 < count:
                at = SUB * j
                pb_ref[at : at + SUB, :] = near[k + 1][j]
                for m in range(SUB):
                    ahead[m] = ahead[m] - near[k + 1][j] * row_copy(pb_ref, at + m)
            r[j] = r[j] * inv[j]
            for m in range(j + 1, SUB):
                r[m] = r[m] - low[m][j] * r[j]
        for j in range(SUB):
            s_ref[base + j : base + j + 1, :] = r[j][0:1, :]
        if k + 3 < count:
            z = list(r)
            for j in range(SUB - 1, -1, -1):
                z[j] = z[j] * inv[j]
                for m in range(j):
                    z[m] = z[m] - low[j][m] * z[j]
        for i in range(k + 1, count):
            left, right = (near[i], r) if i in near else (raw[i], z)
            total = jnp.where(diag, 0.0, rows(i))
            for j in range(SUB):
                total = total - left[j] * right[j]
            s_ref[SUB * i : SUB * (i + 1), :] = total


def extend(base_ref, piv_ref, pe, pf, eo, fo, res_ref, out_ref, ro_ref, t_ref, q_ref, s_ref, cb_ref, pb_ref, sq_ref):
    width = pe.shape[0]
    own = eo.shape[0]
    scale = 1.0 / pe.shape[1]
    pivot_lanes = norm_lanes(pe[...], False)
    pf_split = split2(pf[...])
    for start in range(0, width, TILE):
        part = slice(start, start + TILE)
        expo = dot(pe[part, :], pe[...], NT) + dot(norm_lanes(pe[part, :], True), pivot_lanes, NT)
        row = start + lax.broadcasted_iota(jnp.int32, (TILE, width), 0)
        col = lax.broadcasted_iota(jnp.int32, (TILE, width), 1)
        value = jnp.exp(expo * scale) + jnp.where(row == col, ridge_weight, 0.0)
        t_ref[part, :] = value - dot3(split2(pf[part, :]), pf_split, NT)
    for start in range(0, own, TILE):
        part = slice(start, start + TILE)
        expo = dot(eo[part, :], pe[...], NT) + dot(norm_lanes(eo[part, :], True), pivot_lanes, NT)
        row = base_ref[0] + start + lax.broadcasted_iota(jnp.int32, (TILE, width), 0)
        value = jnp.exp(expo * scale) + jnp.where(row == piv_ref[...], ridge_weight, 0.0)
        q_ref[part, :] = value - dot3(split2(fo[part, :]), pf_split, NT)
    sq_ref[...] = jnp.zeros_like(sq_ref)
    count = width // TILE

    def outer(block, carry):
        at = pl.multiple_of(block * TILE, TILE)
        here = pl.ds(at, TILE)
        s_ref[...] = t_ref[here, here]
        factor_tile(s_ref, cb_ref, pb_ref)
        tall = lax.broadcasted_iota(jnp.int32, (TILE, TILE), 0)
        wide = lax.broadcasted_iota(jnp.int32, (TILE, TILE), 1)
        inverse = split2(jnp.where(wide <= tall, s_ref[...], 0.0))
        upper = split2(dot3(inverse, split2(t_ref[here, :]), NN))
        t_ref[...] -= dot3(upper, upper, TN)
        fresh = dot3(split2(q_ref[:, here]), inverse, NT)
        half = lax.rem(block, count // 2)
        out_ref[block // (count // 2), :, pl.ds(pl.multiple_of(half * TILE, TILE), TILE)] = fresh
        sq_ref[...] += fresh * fresh
        q_ref[...] -= dot3(split2(fresh), upper, NN)
        return carry

    lax.fori_loop(0, count, outer, 0)
    hi, low = split2(sq_ref[...])
    ones = jnp.ones((SUB, TILE), BF16)
    removed = dot(ones, hi, NT) + dot(ones, low, NT)
    ro_ref[...] = res_ref[...] - removed[0:1, :]


def extend_call(base, pivots, pe, pf, eo, fo, residual, interpret=False):
    width, depth = pe.shape
    own, rank = fo.shape
    vmem = pl.BlockSpec(memory_space=pltpu.VMEM)
    return pl.pallas_call(
        extend,
        out_shape=(
            jax.ShapeDtypeStruct((2, own, width // 2), F32),
            jax.ShapeDtypeStruct((1, own), F32),
        ),
        in_specs=[pl.BlockSpec(memory_space=pltpu.SMEM)] + [vmem] * 6,
        out_specs=(vmem, vmem),
        scratch_shapes=[
            pltpu.VMEM((width, width), F32),
            pltpu.VMEM((own, width), F32),
            pltpu.VMEM((TILE, TILE), F32),
            pltpu.VMEM((SUB * SUB, TILE), F32),
            pltpu.VMEM((SUB * SUB, TILE), F32),
            pltpu.VMEM((own, TILE), F32),
        ],
        compiler_params=pltpu.CompilerParams(vmem_limit_bytes=40 * 1024 * 1024),
        name="extend",
        interpret=interpret,
    )(base, pivots, pe, pf, eo, fo, residual)


def shards(embeddings, factor, residual_diag, pivots):
    local_rows, feat_cols = embeddings.shape
    half_rows = factor.shape[0]
    row_group = lax.axis_index("rows")
    feat_group = lax.axis_index("feat")
    rows_start = row_group * local_rows
    half_start = rows_start + feat_group * half_rows
    flat = pivots.reshape(-1)
    owner = flat // local_rows
    prev = jnp.concatenate([jnp.full((2, 1), -1, jnp.int32), owner.reshape(2, -1)[:, :-1]], axis=1).reshape(-1)
    rank = (owner == prev).astype(jnp.int32)
    block_of = jnp.arange(flat.shape[0]) // pivots.shape[1]
    slot = block_of * 2 + rank
    mine = (owner == row_group)
    slot_id = jnp.sum(jnp.where(mine[None, :] & (slot[None, :] == jnp.arange(4)[:, None]), flat[None, :] + 1, 0), axis=1) - 1
    off = slot_id - rows_start
    have = slot_id >= 0
    emb = jnp.where(have[:, None], jnp.take(embeddings, jnp.clip(off, 0, local_rows - 1), axis=0), 0)
    hoff = off - feat_group * half_rows
    hhave = have & (hoff >= 0) & (hoff < half_rows)
    fac = jnp.where(hhave[:, None], jnp.take(factor, jnp.clip(hoff, 0, half_rows - 1), axis=0), 0)
    slots = jnp.concatenate([emb.astype(F32), fac], axis=1)
    every = lax.all_gather(slots, ("rows", "feat"))
    every = every.reshape(-1, 2, 4, slots.shape[1])
    cols = jnp.concatenate([every[:, 0, :, :feat_cols], every[:, 1, :, :feat_cols], every[:, 0, :, feat_cols:] + every[:, 1, :, feat_cols:]], axis=-1).reshape(-1, 2 * feat_cols + 256)
    hot = ((owner * 4 + slot)[:, None] == jnp.arange(cols.shape[0])[None, :]).astype(F32)
    picked = jnp.dot(hot, cols, precision=lax.Precision.HIGHEST)
    pe = picked[:, : 2 * feat_cols].astype(BF16)
    pf = picked[:, 2 * feat_cols :]
    eo = lax.all_to_all(embeddings, "feat", 0, 1, tiled=True)
    base = half_start.reshape(1).astype(jnp.int32)
    fresh, removed = extend_call(base, flat.reshape(1, -1), pe, pf, eo, factor, residual_diag.reshape(1, -1))
    return fresh, removed.reshape(-1)


def solution(mesh):
    return jax.shard_map(
        shards,
        mesh=mesh,
        in_specs=(P("rows", "feat"), P(("rows", "feat"), None), P(("rows", "feat")), P()),
        out_specs=(P(None, ("rows", "feat"), None), P(("rows", "feat"))),
        check_vma=False,
    )
```

time: 708 us -> 190 us (0.27); the launches traced: 698 us -> 189 us
  waiting for transfers between devices: 414 us -> 115 us
  blocking collectives: 117 us -> 0 us
  other arithmetic: 114 us -> 4.75 us
  Pallas kernels: 0 us -> 24.4 us
  starting transfers between devices: 0.17 us -> 10.4 us
  matrix products: 13.8 us -> 5.65 us
    psum x2 -> x0, waiting for transfers between devices: 414 us -> none  [shards(): pivot_factor = lax.psum(own_factor, ('rows', 'feat'))]
    all_gather x0 -> x1, waiting for transfers between devices: none -> 115 us  [shards(): every = lax.all_gather(slots, ('rows', 'feat'))]
    psum x1 -> x0, blocking collectives: 114 us -> none  [shards(): summed_rows = lax.psum(spread, ('rows', 'feat'))]
    another operation x22 -> x0, other arithmetic: 110 us -> none  [the longest x14 69.3 us: shards(): chol_lower = jnp.linalg.cholesky(pivot_block)]
    pallas_call x0 -> x1, Pallas kernels: none -> 24.4 us  [extend_call(): pl.pallas_call(extend, out_shape=(jax.ShapeDtypeStruct((2, own, width //...]
    all_to_all x0 -> x1, starting transfers between devices: none -> 10.4 us  [shards(): eo = lax.all_to_all(embeddings, 'feat', 0, 1, tiled=True)]
    another operation x21 -> x0, local copies, waits for them, and re-layouts: 8.36 us -> none  [the longest x15 8.21 us: shards(): jax.scipy.linalg.solve_triangular(chol_lower, kernel_panel.T, lower=True)]
  transfers between devices with their start and end apart: 4 -> 2, of which waited for: 2 -> 2; matrix products, arithmetic and copies ran while one was open for 19% -> 0% of each run, Pallas kernels for 0% -> 0%
where the time goes in v1:
time: 190 us; the launch traced here: 189 us
  waiting for transfers between devices  115 us (61%)
  Pallas kernels  24.4 us (13%)
  local copies, waits for them, and re-layouts  14.5 us (8%)
  between operations  14.2 us (7%)
  starting transfers between devices  10.4 us (5%)
  matrix products  5.65 us (3%)
  other arithmetic  4.75 us (2%)
    all_gather x1, waiting for transfers between devices, shards(): every = lax.all_gather(slots, ('rows', 'feat'))  115 us
    pallas_call x1, Pallas kernels, extend_call(): pl.pallas_call(extend, out_shape=(jax.ShapeDtypeStruct((2, own, width //...  24.4 us
    all_to_all x1, starting transfers between devices, shards(): eo = lax.all_to_all(embeddings, 'feat', 0, 1, tiled=True)  10.4 us
    dot_general x1, matrix products, shards(): picked = jnp.dot(hot, cols, precision=lax.Precision.HIGHEST)  5.65 us
    concatenate x2, local copies, waits for them, and re-layouts, shards(): jnp.concatenate([every[:, 0, :, :feat_cols], every[:, 1, :, :feat_cols],...  4.45 us
  transfers between devices with their start and end apart: 2, of which 2 were waited for; matrix products, arithmetic and copies ran while one was open for 0% of the time, Pallas kernels for 0%

profile of v1, /device:TPU:1, one launch (start us, length us, event | category | flops | bytes accessed | tf_op | source)
XLA Modules:
  0.0 189.4 jit_solution(12294836823683677883)
XLA Ops:
  7.2 0.7 broadcast_divide_fusion
  7.9 0.7 compare_and_fusion
  8.7 0.1 pad_bitcast_fusion
  8.8 0.1 select_reduce_fusion
  9.0 1.6 gather_fusion.1
  10.5 1.7 gather_fusion
  12.2 0.1 select_select_fusion
  12.3 0.1 select_convert_fusion
  12.4 0.6 maximum_bitcast_fusion
  13.0 10.4 %all-to-all-start = ((bf16[2,384,384]{2,1,0:T(8,128)(2,1)}), bf16[2,384,384]{2,1,0:T(8,128)(2,1)S(1)}, u32[]{:S(2)}, u32[]{:S(2)}) async-start(bf16[2,384,384]{2,1,0:T(8,128)(2,1)} %bitcast.32), calls=%async_computation | async-start | bytes 1179648 | tf_op jit(solution)/shard_map/all_to_all | solution.py:218
  23.4 0.7 copy.10
  24.1 0.7 all-to-all-done
  24.8 0.1 copy.9
  24.9 114.7 %all-gather.4.cloned.1.call-done = f32[512,4,640]{2,1,0:T(4,128)} async-done(((f32[1,4,640]{2,1,0:T(4,128)}), f32[512,4,640]{2,1,0:T(4,128)}) %all-gather.4.cloned.1.call-update) | async-done | bytes 5242896 | tf_op jit(solution)/shard_map/all_gather | solution.py:211
  139.6 1.8 slice_add_fusion
  141.4 3.6 %fusion.16 = (f32[256,1,4,384]{3,2,1,0:T(4,128)S(1)}, f32[256,1,4,384]{3,2,1,0:T(4,128)}) fusion(f32[256,2,4,640]{3,2,1,0:T(4,128)} %bitcast.30), kind=kLoop, calls=%fused_computation.50 | loop fusion | bytes 6291456 | tf_op jit(solution)/shard_map/slice | solution.py:213
  145.1 1.3 add.127
  146.4 2.8 %concatenate.17 = f32[1024,384]{1,0:T(8,128)} reshape(f32[256,1,4,384]{3,2,1,0:T(4,128)} %get-tuple-element.9) | data formatting | bytes 3145728 | tf_op jit(solution)/shard_map/concatenate | solution.py:213
  149.2 1.7 concatenate.16
  150.9 5.6 %fusion = f32[512,1024]{1,0:T(8,128)S(1)} fusion(f32[1024,256]{1,0:T(8,128)S(1)} %copy-done.1, f32[1024,384]{1,0:T(8,128)} %concatenate.17, f32[1024,384]{1,0:T(8,128)} %concatenate.16, s32[512]{0:T(512)S(1)} %get-tuple-element.10), kind=kOutput, calls=%fused_computation.2 | convolution fusion | flops 6445072384 | bytes 6293504 | tf_op jit(solution)/shard_map/dot_general | solution.py:215
  156.6 0.1 slice.46.pe
  156.7 0.8 copy-done
  157.5 24.4 %extend.1 = (f32[2,384,256]{2,1,0:T(8,128)}, f32[1,384]{1,0:T(1,128)S(1)}) custom-call(s32[1]{0:T(128)} %bitcast.base_ref, s32[1,512]{1,0:T(1,128)S(1)} %bitcast.28, bf16[512,768]{1,0:T(8,128)(2,1)S(1)} %slice.46.pe, f32[512,256]{1,0:T(8,128)S(1)} %slice.40.pf, bf16[384,768]{1,0:T(8,128)(2,1)S(1)} %bitcast.27, f32[384,256]{1,0:T(8,128)S(1)} %copy-done, ...), custom_call_target="tpu_custom_call" | custom-call | tf_op jit(solution)/shard_map/extend/pallas_call | solution.py:167
  182.0 0.6 reduce
  (20 shorter events, 0.2 us)
Async XLA Ops:
  7.2 17.7 %copy-start.2 = (f32[384]{0:T(512)S(1)}, f32[384]{0:T(512)}, u32[]{:S(2)}) copy-start(f32[384]{0:T(512)} %param.6) | copy-start | bytes 4612
  7.2 132.4 %all-gather.4.cloned.1.call-start = ((), (), s32[]{:S(2)}) async-start(), calls=%async_computation.1 | async-start | bytes 5253120 | tf_op jit(solution)/shard_map/all_gather | solution.py:211
  13.0 11.8 %all-to-all-start = ((bf16[2,384,384]{2,1,0:T(8,128)(2,1)}), bf16[2,384,384]{2,1,0:T(8,128)(2,1)S(1)}, u32[]{:S(2)}, u32[]{:S(2)}) async-start(bf16[2,384,384]{2,1,0:T(8,128)(2,1)} %bitcast.32), calls=%async_computation | async-start | bytes 1179648 | tf_op jit(solution)/shard_map/all_to_all | solution.py:218
  149.2 1.7 copy-start.1
  156.5 1.0 copy-start
Sparse Core Ops, SparseCore 0:
  13.1 126.4 all-gather.3

commit v2 on v1

--- a/solution.py
+++ b/solution.py
@@ -11,6 +11,10 @@
 BF16 = jnp.bfloat16
 ridge_weight = 2.0
 TILE = 128
+CAP = 2
+X_SIDE = 4
+SIDE = 8
+MESH = pl.DeviceIdType.MESH
 SUB = 8
 
 
@@ -32,13 +36,11 @@
     return dot(a[0], b[0], dims) + (dot(a[0], b[1], dims) + dot(a[1], b[0], dims))
 
 
-def norm_lanes(rows, first):
-    wide = rows.astype(F32)
-    neg = jnp.sum(wide * wide, axis=1, keepdims=True) * -0.5
+def norm_lanes(neg, first):
     hi = neg.astype(BF16).astype(F32)
     mid = (neg - hi).astype(BF16).astype(F32)
     low = (neg - hi) - mid
-    lane = lax.broadcasted_iota(jnp.int32, (rows.shape[0], TILE), 1)
+    lane = lax.broadcasted_iota(jnp.int32, (neg.shape[0], TILE), 1)
     at = 0 if first else 3
     out = jnp.where(lane < 6, 1.0, 0.0)
     out = jnp.where(lane == at, hi, out)
@@ -114,25 +116,281 @@
             s_ref[SUB * i : SUB * (i + 1), :] = total
 
 
-def extend(base_ref, piv_ref, pe, pf, eo, fo, res_ref, out_ref, ro_ref, t_ref, q_ref, s_ref, cb_ref, pb_ref, sq_ref):
+def places(sides):
+    x_side, side = sides
+    r = lax.axis_index("rows")
+    core = lax.axis_index("feat")
+    x = r // (side * side)
+    z = lax.rem(r // side, side)
+    y = lax.rem(r, side)
+    first = z + core * (y - z)
+    other = y + core * (z - y)
+    first_step = side + core * (1 - side)
+    other_step = 1 + core * (side - 1)
+    return r, core, x, first, other, first_step, other_step
+
+
+def gather(sides, emb, fac, piv, a_ref, b_ref, eo_ref, g_ref, h_ref, sx_ref, s1, r1, sc, rc, s2a, r2a, s2b, r2b, s3a, r3a, s3b, r3b, sfa, rfa, sfb, rfb, se, re):
+    x_side, side = sides
+    r, core, x, first, other, first_step, other_step = places(sides)
+    sib = 1 - core
+    cols = emb.shape[1]
+    half = fac.shape[0]
+    rank = fac.shape[1] // 2
+    group = 2 * CAP
+
+    def along_first(i):
+        return r + (i - first) * first_step
+
+    def along_other(i):
+        return r + (i - other) * other_step
+
+    def along_x(i):
+        return r + (i - x) * (side * side)
+
+    def turn(at, step, size):
+        return lax.rem(at + step, size)
+
+    barrier = pltpu.get_barrier_semaphore()
+
+    def greet(row, at):
+        pl.semaphore_signal(barrier, inc=1, device_id=(row, at), device_id_type=MESH)
+
+    greet(r, sib)
+    for d in range(1, side):
+        greet(along_first(turn(first, d, side)), core)
+        greet(along_other(turn(other, d, side)), core)
+        greet(along_first(turn(first, d, side)), sib)
+        greet(along_other(turn(other, d, side)), sib)
+    for d in range(1, x_side):
+        greet(along_x(turn(x, d, x_side)), core)
+
+    start = r * emb.shape[0]
+    ids = []
+    for block in range(2):
+        width = piv.shape[1] // 2
+        chosen = piv[:, block * width : (block + 1) * width]
+        mine = (chosen >= start) & (chosen < start + emb.shape[0])
+        least = jnp.min(jnp.where(mine, chosen, 1 << 30), axis=1, keepdims=True)
+        most = jnp.max(jnp.where(mine, chosen, -1), axis=1, keepdims=True)
+        ids += [least, jnp.where(most == least, -1, most)]
+
+    def picks(count, offset, odd):
+        sub = lax.broadcasted_iota(jnp.int32, (2 * SUB, count), 0) - group * odd
+        row = lax.broadcasted_iota(jnp.int32, (2 * SUB, count), 1) + offset
+        hot = jnp.zeros((2 * SUB, count), F32)
+        for s, one in enumerate(ids):
+            hot = jnp.where((sub == s) & (row == one), 1.0, hot)
+        return hot.astype(BF16)
+
+    odd_first = lax.rem(first, 2)
+    odd_other = lax.rem(other, 2)
+    half_start = start + core * half
+    g_ref[first, :, :cols] = dot(picks(emb.shape[0], start, odd_first), emb[...], NN)[:SUB]
+    wide = fac[...]
+    top = wide.astype(BF16)
+    mid = (wide - top.astype(F32)).astype(BF16)
+
+    def fac_rows(odd):
+        hot = picks(half, half_start, odd)
+        return (dot(hot, top, NN) + dot(hot, mid, NN))[:SUB]
+
+    here = fac_rows(odd_first)
+    there = fac_rows(odd_other)
+    low_half = core == 0
+    g_ref[first, :, cols:] = jnp.where(low_half, here[:, :rank], here[:, rank:])
+    sx_ref[...] = jnp.where(low_half, there[:, rank:], there[:, :rank])
+
+    pl.semaphore_wait(barrier, 4 * (side - 1) + 1 + x_side - 1)
+
+    def copy(src, dst, send, recv, row, at):
+        return pltpu.make_async_remote_copy(
+            src_ref=src, dst_ref=dst, send_sem=send, recv_sem=recv, device_id=(row, at), device_id_type=MESH
+        )
+
+    sends = []
+
+    def go(*args):
+        one = copy(*args)
+        one.start()
+        sends.append(one)
+
+    for d in range(1, side):
+        to = along_first(turn(first, d, side))
+        go(g_ref.at[first], g_ref.at[first], s1.at[d], r1.at[first], to, core)
+    for d in range(side):
+        to = along_other(turn(other, d, side))
+        go(sx_ref, h_ref.at[other], sc.at[d], rc.at[other], to, sib)
+    go(emb.at[pl.ds(pl.multiple_of(sib * half, half), half)], eo_ref, se, re, r, sib)
+    for d in range(1, side):
+        i = turn(first, d, side)
+        copy(g_ref.at[i], g_ref.at[i], s1.at[d], r1.at[i], r, sib).wait_recv()
+    for p in range(side // 2):
+        rows = slice(SUB * p, SUB * (p + 1))
+        both = g_ref[2 * p, :, :cols] + g_ref[2 * p + 1, :, :cols]
+        if p % 2 == 0:
+            held = both
+        else:
+            a_ref[0, x, other, SUB * (p - 1) : SUB * (p + 1), :] = jnp.concatenate([held, both], axis=0).astype(BF16)
+    for d in range(1, side):
+        to = along_other(turn(other, d, side))
+        go(a_ref.at[0, x, other], a_ref.at[0, x, other], s2a.at[d], r2a.at[other], to, core)
+    for i in range(side):
+        copy(sx_ref, h_ref.at[i], sc.at[0], rc.at[i], r, sib).wait_recv()
+    for p in range(0, side // 2, 2):
+        both = [
+            (g_ref[2 * q, :, cols:] + g_ref[2 * q + 1, :, cols:]) + (h_ref[2 * q] + h_ref[2 * q + 1]) for q in (p, p + 1)
+        ]
+        both = jnp.concatenate(both, axis=0)
+        top = both.astype(BF16)
+        rows = slice(SUB * p, SUB * (p + 2))
+        b_ref[0, other, x, rows, :rank] = top
+        b_ref[0, other, x, rows, rank:] = (both - top.astype(F32)).astype(BF16)
+    for d in range(1, x_side):
+        to = along_x(turn(x, d, x_side))
+        go(b_ref.at[0, other, x], b_ref.at[0, other, x], s2b.at[d], r2b.at[x], to, core)
+
+    for d in range(1, side):
+        i = turn(other, d, side)
+        copy(a_ref.at[0, x, i], a_ref.at[0, x, i], s2a.at[d], r2a.at[i], r, sib).wait_recv()
+    for d in range(1, x_side):
+        to = along_x(turn(x, d, x_side))
+        go(a_ref.at[0, x], a_ref.at[0, x], s3a.at[d], r3a.at[x], to, core)
+    for d in range(1, x_side):
+        i = turn(x, d, x_side)
+        copy(b_ref.at[0, other, i], b_ref.at[0, other, i], s2b.at[d], r2b.at[i], r, sib).wait_recv()
+    for d in range(1, side):
+        to = along_other(turn(other, d, side))
+        go(b_ref.at[0, other], b_ref.at[0, other], s3b.at[d], r3b.at[other], to, core)
+
+    go(a_ref.at[0, x], a_ref.at[1, x], sfa.at[0], rfa.at[x], r, sib)
+    go(b_ref.at[0, other], b_ref.at[1, other], sfb.at[0], rfb.at[other], r, sib)
+    for d in range(1, side):
+        i = turn(other, d, side)
+        copy(b_ref.at[0, i], b_ref.at[0, i], s3b.at[d], r3b.at[i], r, sib).wait_recv()
+        go(b_ref.at[0, i], b_ref.at[1, i], sfb.at[d], rfb.at[i], r, sib)
+    for d in range(1, x_side):
+        i = turn(x, d, x_side)
+        copy(a_ref.at[0, i], a_ref.at[0, i], s3a.at[d], r3a.at[i], r, sib).wait_recv()
+        go(a_ref.at[0, i], a_ref.at[1, i], sfa.at[d], rfa.at[i], r, sib)
+    for i in range(side):
+        copy(b_ref.at[0, i], b_ref.at[1, i], sfb.at[i], rfb.at[i], r, sib).wait_recv()
+    for i in range(x_side):
+        copy(a_ref.at[0, i], a_ref.at[1, i], sfa.at[i], rfa.at[i], r, sib).wait_recv()
+    copy(eo_ref, eo_ref, se, re, r, sib).wait_recv()
+    for one in sends:
+        one.wait_send()
+
+
+def gather_call(emb, fac, piv, sides=(X_SIDE, SIDE)):
+    x_side, side = sides
+    vmem = pl.BlockSpec(memory_space=pltpu.VMEM)
+    group = side * 2 * CAP
+    cols, rank = emb.shape[1], fac.shape[1]
+    dma = pltpu.SemaphoreType.DMA
+    counts = [side, side, side, side, side, side, x_side, x_side, x_side, x_side, side, side, x_side, x_side, side, side]
+    return pl.pallas_call(
+        functools.partial(gather, sides),
+        out_shape=(
+            jax.ShapeDtypeStruct((2, x_side, side, group, cols), BF16),
+            jax.ShapeDtypeStruct((2, side, x_side, group, rank), BF16),
+            jax.ShapeDtypeStruct((fac.shape[0], cols), BF16),
+        ),
+        in_specs=[vmem] * 3,
+        out_specs=(vmem,) * 3,
+        scratch_shapes=[
+            pltpu.VMEM((side, SUB, cols + rank // 2), F32),
+            pltpu.VMEM((side, SUB, rank // 2), F32),
+            pltpu.VMEM((SUB, rank // 2), F32),
+        ]
+        + [dma((n,)) for n in counts]
+        + [dma, dma],
+        compiler_params=pltpu.CompilerParams(
+            collective_id=0, has_side_effects=True, vmem_limit_bytes=32 * 1024 * 1024
+        ),
+        name="gather_pivots",
+    )(emb, fac, piv)
+
+
+def slot_rows(piv, local_rows, sides, core, part_x_first):
+    x_side, side = sides
+    width = piv.shape[1]
+    owner = ((piv.astype(F32) + 0.5) * (1.0 / local_rows)).astype(jnp.int32)
+    lane = lax.broadcasted_iota(jnp.int32, piv.shape, 1)
+    second = lane >= width // 2
+    before = pltpu.roll(jnp.broadcast_to(owner, (SUB, width)), 1, axis=1)[0:1, :]
+    again = (before == owner) & (lane != 0) & (lane != width // 2)
+    slot = jnp.where(second, CAP, 0) + jnp.where(again, 1, 0)
+    bits = side.bit_length() - 1
+    y = owner & (side - 1)
+    z = (owner >> bits) & (side - 1)
+    x = owner >> (2 * bits)
+    first = jnp.where(core == 0, z, y)
+    other = jnp.where(core == 0, y, z)
+    outer = x * side + other if part_x_first else other * x_side + x
+    flat = ((outer * side + first) * (2 * CAP) + slot).astype(F32)
+    tiles = [
+        jnp.transpose(jnp.broadcast_to(flat[:, at : at + TILE], (TILE, TILE))) for at in range(0, width, TILE)
+    ]
+    return tiles
+
+
+def pick_rows(src, tiles, dst):
+    count = src.shape[0]
+    data = src[...]
+    for t, tile in enumerate(tiles):
+        lane = lax.broadcasted_iota(jnp.int32, (TILE, TILE), 1).astype(F32)
+        hot = jnp.concatenate(
+            [jnp.where(tile == lane + float(at), 1.0, 0.0).astype(BF16) for at in range(0, count, TILE)], axis=1
+        )
+        dst[t * TILE : (t + 1) * TILE, :] = dot(hot, data, NN).astype(BF16)
+
+
+def extend(sides, base_ref, piv_ref, a_ref, b_ref, emb, es, fo, res_ref, out_ref, ro_ref, pe, ps, pf, fs, t_ref, q_ref, s_ref, cb_ref, pb_ref, sq_ref):
+    core = base_ref[1]
     width = pe.shape[0]
-    own = eo.shape[0]
-    scale = 1.0 / pe.shape[1]
-    pivot_lanes = norm_lanes(pe[...], False)
-    pf_split = split2(pf[...])
+    own = es.shape[0]
+    cols = es.shape[1]
+    rank = fo.shape[1]
+    scale = 1.0 / (2 * cols)
+    for at, at_core, emb_out, fac_out in ((0, core, pe, pf), (1, 1 - core, ps, fs)):
+        pick_rows(a_ref.at[at], slot_rows(piv_ref[...], emb.shape[0], sides, at_core, True), emb_out)
+        pick_rows(b_ref.at[at], slot_rows(piv_ref[...], emb.shape[0], sides, at_core, False), fac_out)
+
+    def norms(one, two):
+        one, two = one.astype(F32), two.astype(F32)
+        return jnp.sum(one * one + two * two, axis=1, keepdims=True) * -0.5
+
+    def fac_dot(left, right):
+        h = rank // 2
+        lhs = jnp.concatenate([left[0], left[0], left[1]], axis=1)
+        return dot(lhs, right, NT)
+
+    h = rank // 2
+    right = jnp.concatenate(
+        [pf[:, :h], fs[:, :h], pf[:, h:], fs[:, h:], pf[:, :h], fs[:, :h]], axis=1
+    )
+    pivot_lanes = norm_lanes(norms(pe[...], ps[...]), False)
     for start in range(0, width, TILE):
         part = slice(start, start + TILE)
-        expo = dot(pe[part, :], pe[...], NT) + dot(norm_lanes(pe[part, :], True), pivot_lanes, NT)
+        expo = dot(pe[part, :], pe[...], NT) + dot(ps[part, :], ps[...], NT)
+        expo += dot(norm_lanes(norms(pe[part, :], ps[part, :]), True), pivot_lanes, NT)
         row = start + lax.broadcasted_iota(jnp.int32, (TILE, width), 0)
         col = lax.broadcasted_iota(jnp.int32, (TILE, width), 1)
         value = jnp.exp(expo * scale) + jnp.where(row == col, ridge_weight, 0.0)
-        t_ref[part, :] = value - dot3(split2(pf[part, :]), pf_split, NT)
+        high = jnp.concatenate([pf[part, :h], fs[part, :h]], axis=1)
+        low = jnp.concatenate([pf[part, h:], fs[part, h:]], axis=1)
+        t_ref[part, :] = value - fac_dot((high, low), right)
     for start in range(0, own, TILE):
         part = slice(start, start + TILE)
-        expo = dot(eo[part, :], pe[...], NT) + dot(norm_lanes(eo[part, :], True), pivot_lanes, NT)
+        mine = emb[pl.ds(pl.multiple_of(core * own + start, TILE), TILE), :]
+        expo = dot(mine, pe[...], NT) + dot(es[part, :], ps[...], NT)
+        expo += dot(norm_lanes(norms(mine, es[part, :]), True), pivot_lanes, NT)
         row = base_ref[0] + start + lax.broadcasted_iota(jnp.int32, (TILE, width), 0)
         value = jnp.exp(expo * scale) + jnp.where(row == piv_ref[...], ridge_weight, 0.0)
-        q_ref[part, :] = value - dot3(split2(fo[part, :]), pf_split, NT)
+        near = fo[part, pl.ds(pl.multiple_of(core * h, h), h)]
+        far = fo[part, pl.ds(pl.multiple_of((1 - core) * h, h), h)]
+        q_ref[part, :] = value - fac_dot(split2(jnp.concatenate([near, far], axis=1)), right)
     sq_ref[...] = jnp.zeros_like(sq_ref)
     count = width // TILE
 
@@ -160,19 +418,24 @@
     ro_ref[...] = res_ref[...] - removed[0:1, :]
 
 
-def extend_call(base, pivots, pe, pf, eo, fo, residual, interpret=False):
-    width, depth = pe.shape
+def extend_call(base, pivots, a, b, emb, es, fo, residual, sides=(X_SIDE, SIDE)):
+    width = pivots.shape[1]
     own, rank = fo.shape
+    cols = emb.shape[1]
     vmem = pl.BlockSpec(memory_space=pltpu.VMEM)
     return pl.pallas_call(
-        extend,
+        functools.partial(extend, sides),
         out_shape=(
             jax.ShapeDtypeStruct((2, own, width // 2), F32),
             jax.ShapeDtypeStruct((1, own), F32),
         ),
-        in_specs=[pl.BlockSpec(memory_space=pltpu.SMEM)] + [vmem] * 6,
+        in_specs=[pl.BlockSpec(memory_space=pltpu.SMEM)] + [vmem] * 7,
         out_specs=(vmem, vmem),
         scratch_shapes=[
+            pltpu.VMEM((width, cols), BF16),
+            pltpu.VMEM((width, cols), BF16),
+            pltpu.VMEM((width, rank), BF16),
+            pltpu.VMEM((width, rank), BF16),
             pltpu.VMEM((width, width), F32),
             pltpu.VMEM((own, width), F32),
             pltpu.VMEM((TILE, TILE), F32),
@@ -182,48 +445,26 @@
         ],
         compiler_params=pltpu.CompilerParams(vmem_limit_bytes=40 * 1024 * 1024),
         name="extend",
-        interpret=interpret,
-    )(base, pivots, pe, pf, eo, fo, residual)
-
-
-def shards(embeddings, factor, residual_diag, pivots):
-    local_rows, feat_cols = embeddings.shape
-    half_rows = factor.shape[0]
-    row_group = lax.axis_index("rows")
-    feat_group = lax.axis_index("feat")
-    rows_start = row_group * local_rows
-    half_start = rows_start + feat_group * half_rows
-    flat = pivots.reshape(-1)
-    owner = flat // local_rows
-    prev = jnp.concatenate([jnp.full((2, 1), -1, jnp.int32), owner.reshape(2, -1)[:, :-1]], axis=1).reshape(-1)
-    rank = (owner == prev).astype(jnp.int32)
-    block_of = jnp.arange(flat.shape[0]) // pivots.shape[1]
-    slot = block_of * 2 + rank
-    mine = (owner == row_group)
-    slot_id = jnp.sum(jnp.where(mine[None, :] & (slot[None, :] == jnp.arange(4)[:, None]), flat[None, :] + 1, 0), axis=1) - 1
-    off = slot_id - rows_start
-    have = slot_id >= 0
-    emb = jnp.where(have[:, None], jnp.take(embeddings, jnp.clip(off, 0, local_rows - 1), axis=0), 0)
-    hoff = off - feat_group * half_rows
-    hhave = have & (hoff >= 0) & (hoff < half_rows)
-    fac = jnp.where(hhave[:, None], jnp.take(factor, jnp.clip(hoff, 0, half_rows - 1), axis=0), 0)
-    slots = jnp.concatenate([emb.astype(F32), fac], axis=1)
-    every = lax.all_gather(slots, ("rows", "feat"))
-    every = every.reshape(-1, 2, 4, slots.shape[1])
-    cols = jnp.concatenate([every[:, 0, :, :feat_cols], every[:, 1, :, :feat_cols], every[:, 0, :, feat_cols:] + every[:, 1, :, feat_cols:]], axis=-1).reshape(-1, 2 * feat_cols + 256)
-    hot = ((owner * 4 + slot)[:, None] == jnp.arange(cols.shape[0])[None, :]).astype(F32)
-    picked = jnp.dot(hot, cols, precision=lax.Precision.HIGHEST)
-    pe = picked[:, : 2 * feat_cols].astype(BF16)
-    pf = picked[:, 2 * feat_cols :]
-    eo = lax.all_to_all(embeddings, "feat", 0, 1, tiled=True)
-    base = half_start.reshape(1).astype(jnp.int32)
-    fresh, removed = extend_call(base, flat.reshape(1, -1), pe, pf, eo, factor, residual_diag.reshape(1, -1))
+    )(base, pivots, a, b, emb, es, fo, residual)
+
+
+def shards(sides, embeddings, factor, residual_diag, pivots):
+    local_rows = embeddings.shape[0]
+    half_rows, rank = factor.shape
+    core = lax.axis_index("feat")
+    base = lax.axis_index("rows") * local_rows + core * half_rows
+    flat = pivots.reshape(1, -1)
+    a, b, es = gather_call(embeddings, factor, flat, sides)
+    a = a.reshape(2, -1, embeddings.shape[1])
+    b = b.reshape(2, -1, rank)
+    place = jnp.stack([base, core]).astype(jnp.int32)
+    fresh, removed = extend_call(place, flat, a, b, embeddings, es, factor, residual_diag.reshape(1, -1), sides)
     return fresh, removed.reshape(-1)
 
 
 def solution(mesh):
     return jax.shard_map(
-        shards,
+        functools.partial(shards, (X_SIDE, SIDE)),
         mesh=mesh,
         in_specs=(P("rows", "feat"), P(("rows", "feat"), None), P(("rows", "feat")), P()),
         out_specs=(P(None, ("rows", "feat"), None), P(("rows", "feat"))),

time: 190 us -> 73.8 us (0.39)
  waiting for transfers between devices: 115 us -> 0 us
  Pallas kernels: 24.4 us -> 66.7 us
  between operations: 14.2 us -> 0.66 us
  starting transfers between devices: 10.4 us -> 0 us
  local copies, waits for them, and re-layouts: 14.5 us -> 5.48 us
  matrix products: 5.65 us -> 0 us
  other arithmetic: 4.75 us -> 0.67 us
    all_gather x1 -> x0, waiting for transfers between devices: 115 us -> none  [shards(): every = lax.all_gather(slots, ('rows', 'feat'))]
    pallas_call x1 -> x2, Pallas kernels: 24.4 us -> 66.7 us  [the longest x1 39.8 us: gather_call(): pl.pallas_call(functools.partial(gather, sides), out_shape=(jax.ShapeDtyp...]
    all_to_all x1 -> x0, starting transfers between devices: 10.4 us -> none  [shards(): eo = lax.all_to_all(embeddings, 'feat', 0, 1, tiled=True)]
    dot_general x1 -> x0, matrix products: 5.65 us -> none  [shards(): picked = jnp.dot(hot, cols, precision=lax.Precision.HIGHEST)]
    concatenate x2 -> x0, local copies, waits for them, and re-layouts: 4.45 us -> none  [shards(): jnp.concatenate([every[:, 0, :, :feat_cols], every[:, 1, :, :feat_cols],...]
    slice x3 -> x0, local copies, waits for them, and re-layouts: 3.77 us -> none  [the longest x1 3.63 us: shards(): every[:, 0, :, :feat_cols]]
    gather x2 -> x0, local copies, waits for them, and re-layouts: 3.27 us -> none  [the longest x1 1.71 us: shards(): jnp.take(embeddings, jnp.clip(off, 0, local_rows - 1), axis=0)]
    unnamed x11 -> x9, local copies, waits for them, and re-layouts: 1.62 us -> 4.8 us
  transfers between devices with their start and end apart: 2 -> 0, of which waited for: 2 -> 0; matrix products, arithmetic and copies ran while one was open for 0% -> 0% of each run, Pallas kernels for 0% -> 0%
where the time goes in v2:
time: 73.8 us; the launch traced here: 73.5 us
  Pallas kernels  66.7 us (90%)
  local copies, waits for them, and re-layouts  5.48 us (7%)
    pallas_call x1, Pallas kernels, gather_call(): pl.pallas_call(functools.partial(gather, sides), out_shape=(jax.ShapeDtyp...  39.8 us
    pallas_call x1, Pallas kernels, extend_call(): pl.pallas_call(functools.partial(extend, sides), out_shape=(jax.ShapeDtyp...  26.8 us
    unnamed x9, local copies, waits for them, and re-layouts  4.8 us

profile of v2, /device:TPU:1, one launch (start us, length us, event | category | flops | bytes accessed | tf_op | source)
XLA Modules:
  0.0 73.5 jit_solution(13594611919446564693)
XLA Ops:
  0.6 0.1 pad_add_fusion.base_ref
  0.7 0.7 reshape.22.res_ref
  1.4 0.7 copy.6
  2.1 0.0 copy-start
  2.1 1.1 %copy-done = bf16[768,384]{1,0:T(8,128)(2,1)S(1)} copy-done((bf16[768,384]{1,0:T(8,128)(2,1)S(1)}, bf16[768,384]{1,0:T(8,128)(2,1)}, u32[]{:S(2)}) %copy-start) | copy-done | bytes 589848
  3.1 0.0 copy-start.2
  3.1 1.0 %copy-done.2 = f32[384,256]{1,0:T(8,128)S(1)} copy-done((f32[384,256]{1,0:T(8,128)S(1)}, f32[384,256]{1,0:T(8,128)}, u32[]{:S(2)}) %copy-start.2) | copy-done | bytes 393240
  4.1 39.8 %gather_pivots.1 = (bf16[2,4,8,32,384]{4,3,2,1,0:T(8,128)(2,1)S(1)}, bf16[2,8,4,32,256]{4,3,2,1,0:T(8,128)(2,1)S(1)}, bf16[384,384]{1,0:T(8,128)(2,1)S(1)}) custom-call(bf16[768,384]{1,0:T(8,128)(2,1)S(1)} %copy-done, f32[384,256]{1,0:T(8,128)S(1)} %copy-done.2, s32[1,512]{1,0:T(1,128)S(1)} %bitcast.9), custom_call_target="tpu_custom_call" | custom-call | tf_op jit(solution)/shard_map/gather_pivots/pallas_call | solution.py:292
  44.0 0.0 copy-start.1
  44.0 1.1 %copy-done.1 = bf16[768,384]{1,0:T(8,128)(2,1)S(1)} copy-done((bf16[768,384]{1,0:T(8,128)(2,1)S(1)}, bf16[768,384]{1,0:T(8,128)(2,1)}, u32[]{:S(2)}) %copy-start.1) | copy-done | bytes 589848
  45.0 0.0 copy-start.3
  45.0 1.0 %copy-done.3 = f32[384,256]{1,0:T(8,128)S(1)} copy-done((f32[384,256]{1,0:T(8,128)S(1)}, f32[384,256]{1,0:T(8,128)}, u32[]{:S(2)}) %copy-start.3) | copy-done | bytes 393240
  46.0 26.8 %extend.1 = (f32[2,384,256]{2,1,0:T(8,128)}, f32[1,384]{1,0:T(1,128)S(1)}) custom-call(s32[2]{0:T(128)S(1)} %pad_add_fusion.base_ref, s32[1,512]{1,0:T(1,128)S(1)} %bitcast.10, bf16[2,1024,384]{2,1,0:T(8,128)(2,1)S(1)} %bitcast.7, bf16[2,1024,256]{2,1,0:T(8,128)(2,1)S(1)} %bitcast.8, bf16[768,384]{1,0:T(8,128)(2,1)S(1)} %copy-done.1, ...), custom_call_target="tpu_custom_call" | custom-call | tf_op jit(solution)/shard_map/extend/pallas_call | solution.py:426
  72.9 0.6 reduce
Async XLA Ops:
  2.1 1.1 %copy-start = (bf16[768,384]{1,0:T(8,128)(2,1)S(1)}, bf16[768,384]{1,0:T(8,128)(2,1)}, u32[]{:S(2)}) copy-start(bf16[768,384]{1,0:T(8,128)(2,1)} %emb.3) | copy-start | bytes 1769476
  3.1 1.0 %copy-start.2 = (f32[384,256]{1,0:T(8,128)S(1)}, f32[384,256]{1,0:T(8,128)}, u32[]{:S(2)}) copy-start(f32[384,256]{1,0:T(8,128)} %fo.1) | copy-start | bytes 1179652
  44.0 1.1 %copy-start.1 = (bf16[768,384]{1,0:T(8,128)(2,1)S(1)}, bf16[768,384]{1,0:T(8,128)(2,1)}, u32[]{:S(2)}) copy-start(bf16[768,384]{1,0:T(8,128)(2,1)} %emb.3) | copy-start | bytes 1769476
  45.0 1.0 %copy-start.3 = (f32[384,256]{1,0:T(8,128)S(1)}, f32[384,256]{1,0:T(8,128)}, u32[]{:S(2)}) copy-start(f32[384,256]{1,0:T(8,128)} %fo.1) | copy-start | bytes 1179652

commit v3 on v2

v3 whole, which is shorter than its diff:
```python
import functools

import jax
import jax.numpy as jnp
from jax import lax
from jax.experimental import pallas as pl
from jax.experimental.pallas import tpu as pltpu
from jax.sharding import PartitionSpec as P

F32 = jnp.float32
BF16 = jnp.bfloat16
ridge_weight = 2.0
TILE = 128
CAP = 2
X_SIDE = 4
SIDE = 8
FAC_MAX = 0.1
LEVELS = 32767.0
MESH = pl.DeviceIdType.MESH
SUB = 8


def dot(a, b, dims):
    return lax.dot_general(a, b, (dims, ((), ())), preferred_element_type=F32)


NN = ((1,), (0,))
NT = ((1,), (1,))
TN = ((0,), (0,))


def split2(x):
    hi = x.astype(BF16)
    return hi, (x - hi.astype(F32)).astype(BF16)


def dot3(a, b, dims):
    return dot(a[0], b[0], dims) + (dot(a[0], b[1], dims) + dot(a[1], b[0], dims))


def norm_lanes(neg, first):
    hi = neg.astype(BF16).astype(F32)
    mid = (neg - hi).astype(BF16).astype(F32)
    low = (neg - hi) - mid
    lane = lax.broadcasted_iota(jnp.int32, (neg.shape[0], TILE), 1)
    at = 0 if first else 3
    out = jnp.where(lane < 6, 1.0, 0.0)
    out = jnp.where(lane == at, hi, out)
    out = jnp.where(lane == at + 1, mid, out)
    out = jnp.where(lane == at + 2, low, out)
    return out.astype(BF16)


def factor_tile(s_ref, cb_ref, pb_ref):
    count = TILE // SUB
    shape = (SUB, TILE)
    lane = lax.broadcasted_iota(jnp.int32, shape, 1)

    def rows(i):
        return s_ref[SUB * i : SUB * (i + 1), :]

    def lane_copy(x, at):
        return jnp.broadcast_to(x[:, at : at + 1], shape)

    def row_copy(ref, at):
        return jnp.broadcast_to(ref[at : at + 1, :], shape)

    ahead = [lane_copy(rows(0), j) for j in range(SUB)]
    for k in range(count):
        base = SUB * k
        diag = (lane >= base) & (lane < base + SUB)
        for j in range(SUB):
            cb_ref[SUB * j : SUB * (j + 1), :] = ahead[j]
        a = [[row_copy(cb_ref, SUB * q + m) if q <= m else None for q in range(SUB)] for m in range(SUB)]
        raw = {}
        for i in range(k + 1, count):
            block = rows(i)
            raw[i] = [lane_copy(block, base + j) for j in range(SUB)]
        near = {i: list(raw[i]) for i in range(k + 1, min(k + 3, count))}
        r = [jnp.where(diag, jnp.where(lane == base + j, 1.0, 0.0), row_copy(s_ref, base + j)) for j in range(SUB)]
        if k + 1 < count:
            block = rows(k + 1)
            ahead = [lane_copy(block, base + SUB + j) for j in range(SUB)]
        inv = []
        low = [[None] * SUB for _ in range(SUB)]
        for j in range(SUB):
            inv.append(lax.rsqrt(a[j][j]))
            for m in range(j + 1, SUB):
                low[m][j] = a[m][j] * inv[j]
            for q in range(j + 1, SUB):
                for m in range(q, SUB):
                    a[m][q] = a[m][q] - low[m][j] * low[q][j]
            for i in near:
                near[i][j] = near[i][j] * inv[j]
                for m in range(j + 1, SUB):
                    near[i][m] = near[i][m] - near[i][j] * low[m][j]
            if k + 1 < count:
                at = SUB * j
                pb_ref[at : at + SUB, :] = near[k + 1][j]
                for m in range(SUB):
                    ahead[m] = ahead[m] - near[k + 1][j] * row_copy(pb_ref, at + m)
            r[j] = r[j] * inv[j]
            for m in range(j + 1, SUB):
                r[m] = r[m] - low[m][j] * r[j]
        for j in range(SUB):
            s_ref[base + j : base + j + 1, :] = r[j][0:1, :]
        if k + 3 < count:
            z = list(r)
            for j in range(SUB - 1, -1, -1):
                z[j] = z[j] * inv[j]
                for m in range(j):
                    z[m] = z[m] - low[j][m] * z[j]
        for i in range(k + 1, count):
            left, right = (near[i], r) if i in near else (raw[i], z)
            total = jnp.where(diag, 0.0, rows(i))
            for j in range(SUB):
                total = total - left[j] * right[j]
            s_ref[SUB * i : SUB * (i + 1), :] = total


def places(sides):
    x_side, side = sides
    r = lax.axis_index("rows")
    core = lax.axis_index("feat")
    x = r // (side * side)
    z = lax.rem(r // side, side)
    y = lax.rem(r, side)
    first = z + core * (y - z)
    other = y + core * (z - y)
    first_step = side + core * (1 - side)
    other_step = 1 + core * (side - 1)
    return r, core, x, first, other, first_step, other_step


def gather(sides, emb_any, fac_any, piv, a_ref, b_ref, eo_ref, emb, fac, g_ref, s1, r1, s2a, r2a, s2b, r2b, s3a, r3a, s3b, r3b, sfa, rfa, sfb, rfb, se, re, le, lf):
    x_side, side = sides
    r, core, x, first, other, first_step, other_step = places(sides)
    sib = 1 - core
    cols = emb.shape[1]
    half = fac.shape[0]
    group = 2 * CAP

    load_emb = pltpu.make_async_copy(emb_any, emb, le)
    load_fac = pltpu.make_async_copy(fac_any, fac, lf)
    load_emb.start()
    load_fac.start()

    def along_first(i):
        return r + (i - first) * first_step

    def along_other(i):
        return r + (i - other) * other_step

    def along_x(i):
        return r + (i - x) * (side * side)

    def turn(at, step, size):
        return lax.rem(at + step, size)

    barrier = pltpu.get_barrier_semaphore()

    def greet(row, at):
        pl.semaphore_signal(barrier, inc=1, device_id=(row, at), device_id_type=MESH)

    greet(r, sib)
    for d in range(1, side):
        greet(along_first(turn(first, d, side)), core)
        greet(along_other(turn(other, d, side)), core)
    for d in range(1, x_side):
        greet(along_x(turn(x, d, x_side)), core)

    start = r * emb.shape[0]
    ids = []
    for block in range(2):
        chosen = piv[block : block + 1, :]
        mine = (chosen >= start) & (chosen < start + emb.shape[0])
        least = jnp.min(jnp.where(mine, chosen, 1 << 30), axis=1, keepdims=True)
        most = jnp.max(jnp.where(mine, chosen, -1), axis=1, keepdims=True)
        ids += [least, jnp.where(most == least, -1, most)]

    def picks(count, offset):
        sub = lax.broadcasted_iota(jnp.int32, (2 * SUB, count), 0)
        row = lax.broadcasted_iota(jnp.int32, (2 * SUB, count), 1) + offset
        hot = jnp.zeros((2 * SUB, count), F32)
        for s, one in enumerate(ids):
            hot = jnp.where((sub == s) & (row == one), 1.0, hot)
        return hot.astype(BF16)

    hot_fac = picks(half, start + core * half)
    hot_emb = picks(emb.shape[0], start)
    load_emb.wait()
    g_ref[first, :, :cols] = dot(hot_emb, emb[...], NN)[:SUB]
    load_fac.wait()
    top, mid = split2(fac[...])
    own_fac = (dot(hot_fac, top, NN) + dot(hot_fac, mid, NN))[:SUB] * (LEVELS / FAC_MAX)
    own_fac = jnp.floor(own_fac + 0.5)
    g_ref[first, :, cols:] = jnp.clip(own_fac, -LEVELS, LEVELS)

    pl.semaphore_wait(barrier, 2 * (side - 1) + x_side)

    def copy(src, dst, send, recv, row, at):
        return pltpu.make_async_remote_copy(
            src_ref=src, dst_ref=dst, send_sem=send, recv_sem=recv, device_id=(row, at), device_id_type=MESH
        )

    sends = []

    def go(*args):
        one = copy(*args)
        one.start()
        sends.append(one)

    for d in range(1, side):
        to = along_first(turn(first, d, side))
        go(g_ref.at[first], g_ref.at[first], s1.at[d], r1.at[first], to, core)
    go(emb.at[pl.ds(pl.multiple_of(sib * half, half), half)], eo_ref, se, re, r, sib)
    to_row = lax.broadcasted_iota(jnp.int32, (group * side, SUB * side), 0)
    from_row = lax.broadcasted_iota(jnp.int32, (group * side, SUB * side), 1)
    half_rows = CAP * side
    block = jnp.where(to_row >= half_rows, 1, 0)
    inside = to_row - block * half_rows
    source = (inside >> 1) * SUB + block * CAP + (inside & 1)
    order = jnp.where(from_row == source, 1.0, 0.0).astype(BF16)
    for d in range(1, side):
        i = turn(first, d, side)
        copy(g_ref.at[i], g_ref.at[i], s1.at[d], r1.at[i], r, sib).wait_recv()
    held = g_ref[...].reshape(SUB * side, -1)
    a_ref[0, x, other] = dot(order, held[:, :cols].astype(BF16), NN).astype(BF16)
    for d in range(1, side):
        to = along_other(turn(other, d, side))
        go(a_ref.at[0, x, other], a_ref.at[0, x, other], s2a.at[d], r2a.at[other], to, core)
    top, mid = split2(held[:, cols:])
    ints = dot(order, top, NN) + dot(order, mid, NN)
    b_ref[0, other, x] = ints.astype(jnp.int32).astype(jnp.int16)
    for d in range(1, x_side):
        to = along_x(turn(x, d, x_side))
        go(b_ref.at[0, other, x], b_ref.at[0, other, x], s2b.at[d], r2b.at[x], to, core)

    for d in range(1, side):
        i = turn(other, d, side)
        copy(a_ref.at[0, x, i], a_ref.at[0, x, i], s2a.at[d], r2a.at[i], r, sib).wait_recv()
    for d in range(1, x_side):
        to = along_x(turn(x, d, x_side))
        go(a_ref.at[0, x], a_ref.at[0, x], s3a.at[d], r3a.at[x], to, core)
    for d in range(1, x_side):
        i = turn(x, d, x_side)
        copy(b_ref.at[0, other, i], b_ref.at[0, other, i], s2b.at[d], r2b.at[i], r, sib).wait_recv()
    for d in range(1, side):
        to = along_other(turn(other, d, side))
        go(b_ref.at[0, other], b_ref.at[0, other], s3b.at[d], r3b.at[other], to, core)

    go(a_ref.at[0, x], a_ref.at[1, x], sfa.at[0], rfa.at[x], r, sib)
    go(b_ref.at[0, other], b_ref.at[1, other], sfb.at[0], rfb.at[other], r, sib)
    for d in range(1, side):
        i = turn(other, d, side)
        copy(b_ref.at[0, i], b_ref.at[0, i], s3b.at[d], r3b.at[i], r, sib).wait_recv()
        go(b_ref.at[0, i], b_ref.at[1, i], sfb.at[d], rfb.at[i], r, sib)
    for d in range(1, x_side):
        i = turn(x, d, x_side)
        copy(a_ref.at[0, i], a_ref.at[0, i], s3a.at[d], r3a.at[i], r, sib).wait_recv()
        go(a_ref.at[0, i], a_ref.at[1, i], sfa.at[d], rfa.at[i], r, sib)
    for i in range(side):
        copy(b_ref.at[0, i], b_ref.at[1, i], sfb.at[i], rfb.at[i], r, sib).wait_recv()
    for i in range(x_side):
        copy(a_ref.at[0, i], a_ref.at[1, i], sfa.at[i], rfa.at[i], r, sib).wait_recv()
    copy(eo_ref, eo_ref, se, re, r, sib).wait_recv()
    for one in sends:
        one.wait_send()


def gather_call(emb, fac, piv, sides=(X_SIDE, SIDE)):
    x_side, side = sides
    vmem = pl.BlockSpec(memory_space=pltpu.VMEM)
    anywhere = pl.BlockSpec(memory_space=pl.ANY)
    group = side * 2 * CAP
    cols, rank = emb.shape[1], fac.shape[1]
    dma = pltpu.SemaphoreType.DMA
    counts = [side, side, side, side, x_side, x_side, x_side, x_side, side, side, x_side, x_side, side, side]
    return pl.pallas_call(
        functools.partial(gather, sides),
        out_shape=(
            jax.ShapeDtypeStruct((2, x_side, side, group, cols), BF16),
            jax.ShapeDtypeStruct((2, side, x_side, group, rank), jnp.int16),
            jax.ShapeDtypeStruct((fac.shape[0], cols), BF16),
        ),
        in_specs=[anywhere, anywhere, vmem],
        out_specs=(vmem,) * 3,
        scratch_shapes=[
            pltpu.VMEM(emb.shape, BF16),
            pltpu.VMEM(fac.shape, F32),
            pltpu.VMEM((side, SUB, cols + rank), F32),
        ]
        + [dma((n,)) for n in counts]
        + [dma] * 4,
        compiler_params=pltpu.CompilerParams(
            collective_id=0, has_side_effects=True, vmem_limit_bytes=32 * 1024 * 1024
        ),
        name="gather_pivots",
    )(emb, fac, piv)


def pivot_places(piv, local_rows, sides):
    x_side, side = sides
    width = piv.shape[1]
    owner = ((piv.astype(F32) + 0.5) * (1.0 / local_rows)).astype(jnp.int32)
    lane = lax.broadcasted_iota(jnp.int32, piv.shape, 1)
    before = pltpu.roll(jnp.broadcast_to(owner, (SUB, width)), 1, axis=1)[0:1, :]
    again = jnp.where((before == owner) & (lane != 0) & (lane != width // 2), 1, 0)
    bits = side.bit_length() - 1
    return owner >> (2 * bits), (owner >> bits) & (side - 1), owner & (side - 1), again


def slot_rows(found, sides, core, part_x_first):
    x_side, side = sides
    x, z, y, again = found
    first = jnp.where(core == 0, z, y)
    other = jnp.where(core == 0, y, z)
    outer = x * side + other if part_x_first else other * x_side + x
    flat = ((outer * side + first) * CAP + again).astype(F32)
    return [
        jnp.transpose(jnp.broadcast_to(flat[:, at : at + TILE], (TILE, TILE)))
        for at in range(0, flat.shape[1], TILE)
    ]


def one_hot(tile, count):
    lane = lax.broadcasted_iota(jnp.int32, (TILE, TILE), 1).astype(F32)
    return jnp.concatenate(
        [jnp.where(tile == lane + float(at), 1.0, 0.0).astype(BF16) for at in range(0, count, TILE)], axis=1
    )


def extend(sides, piv_ref, a_ref, b_ref, emb_any, es, fo_any, res_ref, out_any, ro_ref, emb, fo, out_ref, pe, ps, pf, t_ref, q_ref, s_ref, cb_ref, pb_ref, sq_ref, le, lf, so):
    x_side, side = sides
    core = lax.axis_index("feat")
    width = pe.shape[0]
    own, cols = es.shape
    local_rows = emb_any.shape[0]
    rank = fo.shape[1]
    scale = 1.0 / (2 * cols)
    base = lax.axis_index("rows") * local_rows + core * own
    load_emb = pltpu.make_async_copy(emb_any.at[pl.ds(pl.multiple_of(core * own, own), own)], emb, le)
    load_fac = pltpu.make_async_copy(fo_any, fo, lf)
    load_emb.start()
    load_fac.start()
    pivots = jnp.concatenate([piv_ref[0:1, :], piv_ref[1:2, :]], axis=1)
    found = pivot_places(pivots, local_rows, sides)
    each = side * CAP
    slots = x_side * side * each
    per_block = width // 2 // TILE
    for block in range(2):
        rows = slice(block * each, (block + 1) * each)
        emb_own = a_ref[0, :, :, rows, :].reshape(slots, cols)
        emb_sib = a_ref[1, :, :, rows, :].reshape(slots, cols)
        fac_parts = []
        for at in range(2):
            ints = b_ref[at, :, :, rows, :].reshape(slots, rank).astype(jnp.int32).astype(F32)
            fac_parts.append(split2(ints))
        tiles = [
            slot_rows(found, sides, at_core, x_first)
            for x_first in (True, False)
            for at_core in (core, 1 - core)
        ]
        for t in range(block * per_block, (block + 1) * per_block):
            part = slice(t * TILE, (t + 1) * TILE)
            pe[part, :] = dot(one_hot(tiles[0][t], slots), emb_own, NN).astype(BF16)
            ps[part, :] = dot(one_hot(tiles[1][t], slots), emb_sib, NN).astype(BF16)
            ints = None
            for at in range(2):
                hot = one_hot(tiles[2 + at][t], slots)
                got = dot(hot, fac_parts[at][0], NN) + dot(hot, fac_parts[at][1], NN)
                ints = got if ints is None else ints + got
            pf[part, :] = ints * (FAC_MAX / LEVELS)

    def norms(one, two):
        one, two = one.astype(F32), two.astype(F32)
        return jnp.sum(one * one + two * two, axis=1, keepdims=True) * -0.5

    def fac_dot(left, right):
        return dot(jnp.concatenate([left[0], left[0], left[1]], axis=1), right, NT)

    high, low = split2(pf[...])
    right = jnp.concatenate([high, low, high], axis=1)
    pivot_lanes = norm_lanes(norms(pe[...], ps[...]), False)
    for start in range(0, width, TILE):
        part = slice(start, start + TILE)
        expo = dot(pe[part, :], pe[start:, :], NT) + dot(ps[part, :], ps[start:, :], NT)
        expo += dot(norm_lanes(norms(pe[part, :], ps[part, :]), True), pivot_lanes[start:, :], NT)
        row = lax.broadcasted_iota(jnp.int32, (TILE, width - start), 0)
        col = lax.broadcasted_iota(jnp.int32, (TILE, width - start), 1)
        value = jnp.exp(expo * scale) + jnp.where(row == col, ridge_weight, 0.0)
        t_ref[part, start:] = value - fac_dot(split2(pf[part, :]), right[start:, :])
    load_emb.wait()
    load_fac.wait()
    for start in range(0, own, TILE):
        part = slice(start, start + TILE)
        expo = dot(emb[part, :], pe[...], NT) + dot(es[part, :], ps[...], NT)
        expo += dot(norm_lanes(norms(emb[part, :], es[part, :]), True), pivot_lanes, NT)
        row = base + start + lax.broadcasted_iota(jnp.int32, (TILE, width), 0)
        value = jnp.exp(expo * scale) + jnp.where(row == pivots, ridge_weight, 0.0)
        q_ref[part, :] = value - fac_dot(split2(fo[part, :]), right)
    count = width // TILE
    tall = lax.broadcasted_iota(jnp.int32, (TILE, TILE), 0)
    flat = lax.broadcasted_iota(jnp.int32, (TILE, TILE), 1)

    def stack_left(pair, axis):
        return jnp.concatenate([pair[0], pair[0], pair[1]], axis=axis)

    def stack_right(pair, axis):
        return jnp.concatenate([pair[0], pair[1], pair[0]], axis=axis)

    def own_step(block, inverse, upper):
        here = slice(block * TILE, (block + 1) * TILE)
        fresh = dot(stack_left(split2(q_ref[:, here]), 1), stack_right(inverse, 1), NT)
        half, at = divmod(block * TILE, width // 2)
        out_ref[half, :, at : at + TILE] = fresh
        sq_ref[...] = fresh * fresh if block == 0 else sq_ref[...] + fresh * fresh
        if upper is not None:
            q_ref[:, (block + 1) * TILE :] -= dot(stack_left(split2(fresh), 1), stack_right(upper, 0), NN)

    late = None
    stores = [pltpu.make_async_copy(out_ref.at[i], out_any.at[i], so.at[i]) for i in range(2)]
    for block in range(count):
        here = slice(block * TILE, (block + 1) * TILE)
        s_ref[...] = t_ref[here, here]
        factor_tile(s_ref, cb_ref, pb_ref)
        if late is not None:
            own_step(*late)
        inverse = split2(jnp.where(flat <= tall, s_ref[...], 0.0))
        upper = None
        if block + 1 < count:
            rest = slice((block + 1) * TILE, width)
            upper = split2(dot(stack_left(inverse, 1), stack_right(split2(t_ref[here, rest]), 0), NN))
            for i in range(block + 1, count):
                rows = slice(i * TILE, (i + 1) * TILE)
                off = (i - block - 1) * TILE
                left = tuple(u[:, off : off + TILE] for u in upper)
                right = tuple(u[:, off:] for u in upper)
                t_ref[rows, i * TILE :] -= dot(stack_left(left, 0), stack_right(right, 0), TN)
        late = (block, inverse, upper)
        if block == count // 2:
            stores[0].start()
    own_step(*late)
    stores[1].start()
    hi, low = split2(sq_ref[...])
    ones = jnp.ones((SUB, TILE), BF16)
    removed = dot(ones, hi, NT) + dot(ones, low, NT)
    ro_ref[...] = res_ref[...] - removed[0:1, :].reshape(own)
    for one in stores:
        one.wait()


def extend_call(pivots, a, b, emb, es, fo, residual, sides=(X_SIDE, SIDE)):
    width = pivots.size
    own, rank = fo.shape
    cols = emb.shape[1]
    vmem = pl.BlockSpec(memory_space=pltpu.VMEM)
    anywhere = pl.BlockSpec(memory_space=pl.ANY)
    dma = pltpu.SemaphoreType.DMA
    return pl.pallas_call(
        functools.partial(extend, sides),
        out_shape=(
            jax.ShapeDtypeStruct((2, own, width // 2), F32),
            jax.ShapeDtypeStruct((own,), F32),
        ),
        in_specs=[vmem, vmem, vmem, anywhere, vmem, anywhere, vmem],
        out_specs=(anywhere, vmem),
        scratch_shapes=[
            pltpu.VMEM((own, cols), BF16),
            pltpu.VMEM((own, rank), F32),
            pltpu.VMEM((2, own, width // 2), F32),
            pltpu.VMEM((width, cols), BF16),
            pltpu.VMEM((width, cols), BF16),
            pltpu.VMEM((width, rank), F32),
            pltpu.VMEM((width, width), F32),
            pltpu.VMEM((own, width), F32),
            pltpu.VMEM((TILE, TILE), F32),
            pltpu.VMEM((SUB * SUB, TILE), F32),
            pltpu.VMEM((SUB * SUB, TILE), F32),
            pltpu.VMEM((own, TILE), F32),
            dma,
            dma,
            dma((2,)),
        ],
        compiler_params=pltpu.CompilerParams(vmem_limit_bytes=40 * 1024 * 1024),
        name="extend",
    )(pivots, a, b, emb, es, fo, residual)


def shards(sides, embeddings, factor, residual_diag, pivots):
    a, b, es = gather_call(embeddings, factor, pivots, sides)
    return extend_call(pivots, a, b, embeddings, es, factor, residual_diag, sides)


def solution(mesh):
    return jax.shard_map(
        functools.partial(shards, (X_SIDE, SIDE)),
        mesh=mesh,
        in_specs=(P("rows", "feat"), P(("rows", "feat"), None), P(("rows", "feat")), P()),
        out_specs=(P(None, ("rows", "feat"), None), P(("rows", "feat"))),
        check_vma=False,
    )
```

time: 73.8 us -> 64.8 us (0.88)
  Pallas kernels: 66.7 us -> 57.6 us
    pallas_call x1, Pallas kernels: 26.8 us -> 17.2 us  [extend_call(): pl.pallas_call(functools.partial(extend, sides), out_shape=(jax.ShapeDtyp...]
    unnamed x9 -> x14, local copies, waits for them, and re-layouts: 4.8 us -> 6.15 us
where the time goes in v3:
time: 64.8 us; the launch traced here: 64.4 us
  Pallas kernels  57.6 us (89%)
  local copies, waits for them, and re-layouts  6.15 us (9%)
  between operations  0.66 us (1%)
    pallas_call x1, Pallas kernels, gather_call(): pl.pallas_call(functools.partial(gather, sides), out_shape=(jax.ShapeDtyp...  40.4 us
    pallas_call x1, Pallas kernels, extend_call(): pl.pallas_call(functools.partial(extend, sides), out_shape=(jax.ShapeDtyp...  17.2 us
    unnamed x14, local copies, waits for them, and re-layouts  6.15 us

profile of v3, /device:TPU:1, one launch (start us, length us, event | category | flops | bytes accessed | tf_op | source)
XLA Modules:
  0.0 64.4 jit_solution(5057765504638679173)
XLA Ops:
  0.6 0.0 copy-start
  0.6 1.1 %copy-done = bf16[768,384]{1,0:T(8,128)(2,1)S(1)} copy-done((bf16[768,384]{1,0:T(8,128)(2,1)S(1)}, bf16[768,384]{1,0:T(8,128)(2,1)}, u32[]{:S(2)}) %copy-start) | copy-done | bytes 589848
  1.7 0.0 copy-start.2
  1.7 1.0 %copy-done.2 = f32[384,256]{1,0:T(8,128)S(1)} copy-done((f32[384,256]{1,0:T(8,128)S(1)}, f32[384,256]{1,0:T(8,128)}, u32[]{:S(2)}) %copy-start.2) | copy-done | bytes 393240
  2.7 0.0 copy-start.4
  2.7 0.7 %copy-done.4 = s32[2,256]{1,0:T(2,128)S(1)} copy-done((s32[2,256]{1,0:T(2,128)S(1)}, s32[2,256]{1,0:T(2,128)}, u32[]{:S(2)}) %copy-start.4) | copy-done | bytes 2072
  3.4 40.4 %gather_pivots.1 = (bf16[2,4,8,32,384]{4,3,2,1,0:T(8,128)(2,1)S(1)}, s16[2,8,4,32,256]{4,3,2,1,0:T(8,128)(2,1)S(1)}, bf16[384,384]{1,0:T(8,128)(2,1)S(1)}) custom-call(bf16[768,384]{1,0:T(8,128)(2,1)S(1)} %copy-done, f32[384,256]{1,0:T(8,128)S(1)} %copy-done.2, s32[2,256]{1,0:T(2,128)S(1)} %copy-done.4), custom_call_target="tpu_custom_call" | custom-call | tf_op jit(solution)/shard_map/gather_pivots/pallas_call | solution.py:279
  43.8 0.0 copy-start.1
  43.8 1.1 %copy-done.1 = bf16[768,384]{1,0:T(8,128)(2,1)S(1)} copy-done((bf16[768,384]{1,0:T(8,128)(2,1)S(1)}, bf16[768,384]{1,0:T(8,128)(2,1)}, u32[]{:S(2)}) %copy-start.1) | copy-done | bytes 589848
  44.9 0.0 copy-start.3
  44.9 1.0 %copy-done.3 = f32[384,256]{1,0:T(8,128)S(1)} copy-done((f32[384,256]{1,0:T(8,128)S(1)}, f32[384,256]{1,0:T(8,128)}, u32[]{:S(2)}) %copy-start.3) | copy-done | bytes 393240
  45.9 0.0 copy-start.5
  45.9 0.7 %copy-done.5 = s32[2,256]{1,0:T(2,128)S(1)} copy-done((s32[2,256]{1,0:T(2,128)S(1)}, s32[2,256]{1,0:T(2,128)}, u32[]{:S(2)}) %copy-start.5) | copy-done | bytes 2072
  46.5 0.0 copy-start.6
  46.5 0.7 %copy-done.6 = f32[384]{0:T(512)S(1)} copy-done((f32[384]{0:T(512)S(1)}, f32[384]{0:T(512)}, u32[]{:S(2)}) %copy-start.6) | copy-done | bytes 1560
  47.2 17.2 %extend.1 = (f32[2,384,256]{2,1,0:T(8,128)}, f32[384]{0:T(512)}) custom-call(s32[2,256]{1,0:T(2,128)S(1)} %copy-done.5, bf16[2,4,8,32,384]{4,3,2,1,0:T(8,128)(2,1)S(1)} %get-tuple-element.5.a_ref, s16[2,8,4,32,256]{4,3,2,1,0:T(8,128)(2,1)S(1)} %get-tuple-element.6.b_ref, bf16[768,384]{1,0:T(8,128)(2,1)S(1)} %copy-done.1, ...), custom_call_target="tpu_custom_call" | custom-call | tf_op jit(solution)/shard_map/extend/pallas_call | solution.py:460
Async XLA Ops:
  0.6 1.1 %copy-start = (bf16[768,384]{1,0:T(8,128)(2,1)S(1)}, bf16[768,384]{1,0:T(8,128)(2,1)}, u32[]{:S(2)}) copy-start(bf16[768,384]{1,0:T(8,128)(2,1)} %emb_any.3) | copy-start | bytes 1769476
  1.7 1.0 %copy-start.2 = (f32[384,256]{1,0:T(8,128)S(1)}, f32[384,256]{1,0:T(8,128)}, u32[]{:S(2)}) copy-start(f32[384,256]{1,0:T(8,128)} %fo_any.1) | copy-start | bytes 1179652
  2.7 0.7 %copy-start.4 = (s32[2,256]{1,0:T(2,128)S(1)}, s32[2,256]{1,0:T(2,128)}, u32[]{:S(2)}) copy-start(s32[2,256]{1,0:T(2,128)} %piv_ref.1) | copy-start | bytes 6148
  43.8 1.1 %copy-start.1 = (bf16[768,384]{1,0:T(8,128)(2,1)S(1)}, bf16[768,384]{1,0:T(8,128)(2,1)}, u32[]{:S(2)}) copy-start(bf16[768,384]{1,0:T(8,128)(2,1)} %emb_any.3) | copy-start | bytes 1769476
  44.9 1.0 %copy-start.3 = (f32[384,256]{1,0:T(8,128)S(1)}, f32[384,256]{1,0:T(8,128)}, u32[]{:S(2)}) copy-start(f32[384,256]{1,0:T(8,128)} %fo_any.1) | copy-start | bytes 1179652
  45.9 0.7 %copy-start.5 = (s32[2,256]{1,0:T(2,128)S(1)}, s32[2,256]{1,0:T(2,128)}, u32[]{:S(2)}) copy-start(s32[2,256]{1,0:T(2,128)} %piv_ref.1) | copy-start | bytes 6148
  46.5 0.7 %copy-start.6 = (f32[384]{0:T(512)S(1)}, f32[384]{0:T(512)}, u32[]{:S(2)}) copy-start(f32[384]{0:T(512)} %res_ref.1) | copy-start | bytes 4612

commit v4 on v3

--- a/solution.py
+++ b/solution.py
@@ -14,6 +14,7 @@
 CAP = 2
 X_SIDE = 4
 SIDE = 8
+ROOM = 40 * 1024 * 1024
 FAC_MAX = 0.1
 LEVELS = 32767.0
 MESH = pl.DeviceIdType.MESH
@@ -132,7 +133,7 @@
     return r, core, x, first, other, first_step, other_step
 
 
-def gather(sides, emb_any, fac_any, piv, a_ref, b_ref, eo_ref, emb, fac, g_ref, s1, r1, s2a, r2a, s2b, r2b, s3a, r3a, s3b, r3b, sfa, rfa, sfb, rfb, se, re, le, lf):
+def gather(sides, emb_any, fac_any, piv_any, a_ref, b_ref, eo_ref, emb, fac, piv, g_ref, s1, r1, s2a, r2a, s2b, r2b, s3a, r3a, s3b, r3b, sfa, rfa, sfb, rfb, se, re, le, lf, lp):
     x_side, side = sides
     r, core, x, first, other, first_step, other_step = places(sides)
     sib = 1 - core
@@ -142,6 +143,8 @@
 
     load_emb = pltpu.make_async_copy(emb_any, emb, le)
     load_fac = pltpu.make_async_copy(fac_any, fac, lf)
+    load_piv = pltpu.make_async_copy(piv_any, piv, lp)
+    load_piv.start()
     load_emb.start()
     load_fac.start()
 
@@ -170,6 +173,7 @@
         greet(along_x(turn(x, d, x_side)), core)
 
     start = r * emb.shape[0]
+    load_piv.wait()
     ids = []
     for block in range(2):
         chosen = piv[block : block + 1, :]
@@ -236,29 +240,51 @@
         to = along_x(turn(x, d, x_side))
         go(b_ref.at[0, other, x], b_ref.at[0, other, x], s2b.at[d], r2b.at[x], to, core)
 
-    for d in range(1, side):
+    def spread_a(i, slot):
+        for d in range(1, x_side):
+            to = along_x(turn(x, d, x_side))
+            go(a_ref.at[0, x, i], a_ref.at[0, x, i], s3a.at[slot, d], r3a.at[x, i], to, core)
+
+    def spread_b(i, slot):
+        for d in range(1, side):
+            to = along_other(turn(other, d, side))
+            go(b_ref.at[0, other, i], b_ref.at[0, other, i], s3b.at[slot, d], r3b.at[other, i], to, core)
+
+    spread_a(other, 0)
+    spread_b(x, 0)
+    b_turns = [1, x_side - 1] + list(range(2, x_side - 1))
+    a_turns = [d for pair in zip(range(1, side // 2), range(side - 1, side // 2, -1)) for d in pair] + [side // 2]
+    for n, d in enumerate(a_turns):
         i = turn(other, d, side)
         copy(a_ref.at[0, x, i], a_ref.at[0, x, i], s2a.at[d], r2a.at[i], r, sib).wait_recv()
-    for d in range(1, x_side):
-        to = along_x(turn(x, d, x_side))
-        go(a_ref.at[0, x], a_ref.at[0, x], s3a.at[d], r3a.at[x], to, core)
-    for d in range(1, x_side):
-        i = turn(x, d, x_side)
-        copy(b_ref.at[0, other, i], b_ref.at[0, other, i], s2b.at[d], r2b.at[i], r, sib).wait_recv()
-    for d in range(1, side):
-        to = along_other(turn(other, d, side))
-        go(b_ref.at[0, other], b_ref.at[0, other], s3b.at[d], r3b.at[other], to, core)
+        spread_a(i, d)
+        if n % 2 == 1 and n // 2 < len(b_turns):
+            d = b_turns[n // 2]
+            i = turn(x, d, x_side)
+            copy(b_ref.at[0, other, i], b_ref.at[0, other, i], s2b.at[d], r2b.at[i], r, sib).wait_recv()
+            spread_b(i, d)
 
     go(a_ref.at[0, x], a_ref.at[1, x], sfa.at[0], rfa.at[x], r, sib)
     go(b_ref.at[0, other], b_ref.at[1, other], sfb.at[0], rfb.at[other], r, sib)
-    for d in range(1, side):
+
+    def pass_a(d):
+        i = turn(x, d, x_side)
+        for j in range(side):
+            copy(a_ref.at[0, i, j], a_ref.at[0, i, j], s3a.at[0, d], r3a.at[i, j], r, sib).wait_recv()
+        go(a_ref.at[0, i], a_ref.at[1, i], sfa.at[d], rfa.at[i], r, sib)
+
+    def pass_b(d):
         i = turn(other, d, side)
-        copy(b_ref.at[0, i], b_ref.at[0, i], s3b.at[d], r3b.at[i], r, sib).wait_recv()
+        for j in range(x_side):
+            copy(b_ref.at[0, i, j], b_ref.at[0, i, j], s3b.at[0, d], r3b.at[i, j], r, sib).wait_recv()
         go(b_ref.at[0, i], b_ref.at[1, i], sfb.at[d], rfb.at[i], r, sib)
-    for d in range(1, x_side):
-        i = turn(x, d, x_side)
-        copy(a_ref.at[0, i], a_ref.at[0, i], s3a.at[d], r3a.at[i], r, sib).wait_recv()
-        go(a_ref.at[0, i], a_ref.at[1, i], sfa.at[d], rfa.at[i], r, sib)
+
+    for d in a_turns[:4]:
+        pass_b(d)
+    for d in b_turns:
+        pass_a(d)
+    for d in a_turns[4:]:
+        pass_b(d)
     for i in range(side):
         copy(b_ref.at[0, i], b_ref.at[1, i], sfb.at[i], rfb.at[i], r, sib).wait_recv()
     for i in range(x_side):
@@ -271,11 +297,11 @@
 def gather_call(emb, fac, piv, sides=(X_SIDE, SIDE)):
     x_side, side = sides
     vmem = pl.BlockSpec(memory_space=pltpu.VMEM)
-    anywhere = pl.BlockSpec(memory_space=pl.ANY)
+    far = pl.BlockSpec(memory_space=pltpu.HBM)
     group = side * 2 * CAP
     cols, rank = emb.shape[1], fac.shape[1]
     dma = pltpu.SemaphoreType.DMA
-    counts = [side, side, side, side, x_side, x_side, x_side, x_side, side, side, x_side, x_side, side, side]
+    counts = [side, side, side, side, x_side, x_side, (side, x_side), (x_side, side), (x_side, side), (side, x_side), x_side, x_side, side, side]
     return pl.pallas_call(
         functools.partial(gather, sides),
         out_shape=(
@@ -283,17 +309,18 @@
             jax.ShapeDtypeStruct((2, side, x_side, group, rank), jnp.int16),
             jax.ShapeDtypeStruct((fac.shape[0], cols), BF16),
         ),
-        in_specs=[anywhere, anywhere, vmem],
+        in_specs=[far] * 3,
         out_specs=(vmem,) * 3,
         scratch_shapes=[
             pltpu.VMEM(emb.shape, BF16),
             pltpu.VMEM(fac.shape, F32),
+            pltpu.VMEM(piv.shape, jnp.int32),
             pltpu.VMEM((side, SUB, cols + rank), F32),
         ]
-        + [dma((n,)) for n in counts]
-        + [dma] * 4,
+        + [dma(n if isinstance(n, tuple) else (n,)) for n in counts]
+        + [dma] * 5,
         compiler_params=pltpu.CompilerParams(
-            collective_id=0, has_side_effects=True, vmem_limit_bytes=32 * 1024 * 1024
+            collective_id=0, has_side_effects=True, vmem_limit_bytes=ROOM
         ),
         name="gather_pivots",
     )(emb, fac, piv)
@@ -330,7 +357,7 @@
     )
 
 
-def extend(sides, piv_ref, a_ref, b_ref, emb_any, es, fo_any, res_ref, out_any, ro_ref, emb, fo, out_ref, pe, ps, pf, t_ref, q_ref, s_ref, cb_ref, pb_ref, sq_ref, le, lf, so):
+def extend(sides, piv_any, a_ref, b_ref, emb_any, es, fo_any, res_any, out_any, ro_any, piv_ref, res_ref, ro_ref, emb, fo, out_ref, pe, ps, pf, t_ref, q_ref, s_ref, cb_ref, pb_ref, sq_ref, le, lf, lp, lr, so):
     x_side, side = sides
     core = lax.axis_index("feat")
     width = pe.shape[0]
@@ -343,6 +370,11 @@
     load_fac = pltpu.make_async_copy(fo_any, fo, lf)
     load_emb.start()
     load_fac.start()
+    load_piv = pltpu.make_async_copy(piv_any, piv_ref, lp)
+    load_res = pltpu.make_async_copy(res_any, res_ref, lr)
+    load_piv.start()
+    load_res.start()
+    load_piv.wait()
     pivots = jnp.concatenate([piv_ref[0:1, :], piv_ref[1:2, :]], axis=1)
     found = pivot_places(pivots, local_rows, sides)
     each = side * CAP
@@ -445,7 +477,10 @@
     hi, low = split2(sq_ref[...])
     ones = jnp.ones((SUB, TILE), BF16)
     removed = dot(ones, hi, NT) + dot(ones, low, NT)
+    load_res.wait()
     ro_ref[...] = res_ref[...] - removed[0:1, :].reshape(own)
+    stores.append(pltpu.make_async_copy(ro_ref, ro_any, so.at[2]))
+    stores[2].start()
     for one in stores:
         one.wait()
 
@@ -455,7 +490,7 @@
     own, rank = fo.shape
     cols = emb.shape[1]
     vmem = pl.BlockSpec(memory_space=pltpu.VMEM)
-    anywhere = pl.BlockSpec(memory_space=pl.ANY)
+    far = pl.BlockSpec(memory_space=pltpu.HBM)
     dma = pltpu.SemaphoreType.DMA
     return pl.pallas_call(
         functools.partial(extend, sides),
@@ -463,9 +498,12 @@
             jax.ShapeDtypeStruct((2, own, width // 2), F32),
             jax.ShapeDtypeStruct((own,), F32),
         ),
-        in_specs=[vmem, vmem, vmem, anywhere, vmem, anywhere, vmem],
-        out_specs=(anywhere, vmem),
+        in_specs=[far, vmem, vmem, far, vmem, far, far],
+        out_specs=(far, far),
         scratch_shapes=[
+            pltpu.VMEM(pivots.shape, jnp.int32),
+            pltpu.VMEM((own,), F32),
+            pltpu.VMEM((own,), F32),
             pltpu.VMEM((own, cols), BF16),
             pltpu.VMEM((own, rank), F32),
             pltpu.VMEM((2, own, width // 2), F32),
@@ -480,14 +518,17 @@
             pltpu.VMEM((own, TILE), F32),
             dma,
             dma,
-            dma((2,)),
+            dma,
+            dma,
+            dma((3,)),
         ],
-        compiler_params=pltpu.CompilerParams(vmem_limit_bytes=40 * 1024 * 1024),
+        compiler_params=pltpu.CompilerParams(vmem_limit_bytes=ROOM),
         name="extend",
     )(pivots, a, b, emb, es, fo, residual)
 
 
-def shards(sides, embeddings, factor, residual_diag, pivots):
+def shards(sides, *given):
+    embeddings, factor, residual_diag, pivots = (pltpu.with_memory_space_constraint(one, pltpu.HBM) for one in given)
     a, b, es = gather_call(embeddings, factor, pivots, sides)
     return extend_call(pivots, a, b, embeddings, es, factor, residual_diag, sides)
 

time: 64.8 us -> 55.7 us (0.86)
  local copies, waits for them, and re-layouts: 6.15 us -> 0 us
  Pallas kernels: 57.6 us -> 54.7 us
    unnamed x14 -> x0, local copies, waits for them, and re-layouts: 6.15 us -> none
    pallas_call x1, Pallas kernels: 40.4 us -> 37.3 us  [gather_call(): pl.pallas_call(functools.partial(gather, sides), out_shape=(jax.ShapeDtyp...]
where the time goes in v4:
time: 55.7 us; the launch traced here: 55.5 us
  Pallas kernels  54.7 us (98%)
  between operations  0.8 us (1%)
    pallas_call x1, Pallas kernels, gather_call(): pl.pallas_call(functools.partial(gather, sides), out_shape=(jax.ShapeDtyp...  37.3 us
    pallas_call x1, Pallas kernels, extend_call(): pl.pallas_call(functools.partial(extend, sides), out_shape=(jax.ShapeDtyp...  17.4 us

profile of v4, /device:TPU:1, one launch (start us, length us, event | category | flops | bytes accessed | tf_op | source)
XLA Modules:
  0.0 55.5 jit_solution(13178794008094017660)
XLA Ops:
  0.6 37.3 %gather_pivots.1 = (bf16[2,4,8,32,384]{4,3,2,1,0:T(8,128)(2,1)S(1)}, s16[2,8,4,32,256]{4,3,2,1,0:T(8,128)(2,1)S(1)}, bf16[384,384]{1,0:T(8,128)(2,1)S(1)}) custom-call(bf16[768,384]{1,0:T(8,128)(2,1)} %emb_any.3, f32[384,256]{1,0:T(8,128)} %fo_any.1, s32[2,256]{1,0:T(2,128)} %piv_any.3), custom_call_target="tpu_custom_call" | custom-call | tf_op jit(solution)/shard_map/gather_pivots/pallas_call | solution.py:305
  38.0 17.4 %extend.1 = (f32[2,384,256]{2,1,0:T(8,128)}, f32[384]{0:T(512)}) custom-call(s32[2,256]{1,0:T(2,128)} %piv_any.3, bf16[2,4,8,32,384]{4,3,2,1,0:T(8,128)(2,1)S(1)} %get-tuple-element.5.a_ref, s16[2,8,4,32,256]{4,3,2,1,0:T(8,128)(2,1)S(1)} %get-tuple-element.6.b_ref, bf16[768,384]{1,0:T(8,128)(2,1)} %emb_any.3, bf16[384,384]{1,0:T(8,128)(2,1)S(1)} %get-tuple-element.7.es, ...), custom_call_target="tpu_custom_call" | custom-call | tf_op jit(solution)/shard_map/extend/pallas_call | solution.py:495

commit v5 on v4

--- a/solution.py
+++ b/solution.py
@@ -12,6 +12,7 @@
 ridge_weight = 2.0
 TILE = 128
 CAP = 2
+GROUPS = 4
 X_SIDE = 4
 SIDE = 8
 ROOM = 40 * 1024 * 1024
@@ -183,22 +184,33 @@
         ids += [least, jnp.where(most == least, -1, most)]
 
     def picks(count, offset):
-        sub = lax.broadcasted_iota(jnp.int32, (2 * SUB, count), 0)
-        row = lax.broadcasted_iota(jnp.int32, (2 * SUB, count), 1) + offset
-        hot = jnp.zeros((2 * SUB, count), F32)
+        sub = lax.broadcasted_iota(jnp.int32, (GROUPS * group, count), 0) & (group - 1)
+        row = lax.broadcasted_iota(jnp.int32, (GROUPS * group, count), 1) + offset
+        hot = jnp.zeros((GROUPS * group, count), F32)
         for s, one in enumerate(ids):
             hot = jnp.where((sub == s) & (row == one), 1.0, hot)
         return hot.astype(BF16)
 
     hot_fac = picks(half, start + core * half)
     hot_emb = picks(emb.shape[0], start)
-    load_emb.wait()
-    g_ref[first, :, :cols] = dot(hot_emb, emb[...], NN)[:SUB]
     load_fac.wait()
     top, mid = split2(fac[...])
-    own_fac = (dot(hot_fac, top, NN) + dot(hot_fac, mid, NN))[:SUB] * (LEVELS / FAC_MAX)
-    own_fac = jnp.floor(own_fac + 0.5)
-    g_ref[first, :, cols:] = jnp.clip(own_fac, -LEVELS, LEVELS)
+    ints = (dot(hot_fac, top, NN) + dot(hot_fac, mid, NN)) * (LEVELS / FAC_MAX)
+    ints = jnp.clip(jnp.floor(ints + 0.5), -LEVELS, LEVELS)
+    high = ints.astype(BF16).astype(F32)
+    low = ints - high
+    load_emb.wait()
+    taken = dot(hot_emb, emb[...], NN)
+    part = lax.broadcasted_iota(jnp.int32, (GROUPS * group, TILE), 0) // group
+    sources = [taken[:, :TILE], taken[:, 2 * TILE :], high[:, TILE:], low[:, TILE:]]
+    left = sources[0]
+    for n in range(1, GROUPS):
+        left = jnp.where(part == n, sources[n], left)
+    right = jnp.where(part == 0, taken[:, TILE : 2 * TILE], 0.0)
+    right = jnp.where(part == 1, high[:, :TILE], right)
+    right = jnp.where(part == 2, low[:, :TILE], right)
+    g_ref[first, :, :TILE] = left.astype(BF16)
+    g_ref[first, :, TILE:] = right.astype(BF16)
 
     pl.semaphore_wait(barrier, 2 * (side - 1) + x_side)
 
@@ -217,25 +229,26 @@
     for d in range(1, side):
         to = along_first(turn(first, d, side))
         go(g_ref.at[first], g_ref.at[first], s1.at[d], r1.at[first], to, core)
-    go(emb.at[pl.ds(pl.multiple_of(sib * half, half), half)], eo_ref, se, re, r, sib)
-    to_row = lax.broadcasted_iota(jnp.int32, (group * side, SUB * side), 0)
-    from_row = lax.broadcasted_iota(jnp.int32, (group * side, SUB * side), 1)
+    to_row = lax.broadcasted_iota(jnp.int32, (group * side, GROUPS * group * side), 0)
+    from_row = lax.broadcasted_iota(jnp.int32, (group * side, GROUPS * group * side), 1)
     half_rows = CAP * side
     block = jnp.where(to_row >= half_rows, 1, 0)
     inside = to_row - block * half_rows
-    source = (inside >> 1) * SUB + block * CAP + (inside & 1)
-    order = jnp.where(from_row == source, 1.0, 0.0).astype(BF16)
+    source = (inside >> 1) * (GROUPS * group) + block * CAP + (inside & 1)
+    orders = [jnp.where(from_row == source + n * group, 1.0, 0.0).astype(BF16) for n in range(GROUPS)]
     for d in range(1, side):
         i = turn(first, d, side)
         copy(g_ref.at[i], g_ref.at[i], s1.at[d], r1.at[i], r, sib).wait_recv()
-    held = g_ref[...].reshape(SUB * side, -1)
-    a_ref[0, x, other] = dot(order, held[:, :cols].astype(BF16), NN).astype(BF16)
+    held = g_ref[...].reshape(GROUPS * group * side, 2 * TILE)
+    outs = [dot(order, held, NN) for order in orders]
+    a_ref[0, x, other, :, : 2 * TILE] = outs[0].astype(BF16)
+    a_ref[0, x, other, :, 2 * TILE :] = outs[1][:, :TILE].astype(BF16)
     for d in range(1, side):
         to = along_other(turn(other, d, side))
         go(a_ref.at[0, x, other], a_ref.at[0, x, other], s2a.at[d], r2a.at[other], to, core)
-    top, mid = split2(held[:, cols:])
-    ints = dot(order, top, NN) + dot(order, mid, NN)
-    b_ref[0, other, x] = ints.astype(jnp.int32).astype(jnp.int16)
+    ints = (outs[1][:, TILE:] + outs[2][:, TILE:], outs[2][:, :TILE] + outs[3][:, :TILE])
+    for n in range(2):
+        b_ref[0, other, x, :, n * TILE : (n + 1) * TILE] = ints[n].astype(jnp.int32).astype(jnp.int16)
     for d in range(1, x_side):
         to = along_x(turn(x, d, x_side))
         go(b_ref.at[0, other, x], b_ref.at[0, other, x], s2b.at[d], r2b.at[x], to, core)
@@ -252,6 +265,7 @@
 
     spread_a(other, 0)
     spread_b(x, 0)
+    go(emb.at[pl.ds(pl.multiple_of(sib * half, half), half)], eo_ref, se, re, r, sib)
     b_turns = [1, x_side - 1] + list(range(2, x_side - 1))
     a_turns = [d for pair in zip(range(1, side // 2), range(side - 1, side // 2, -1)) for d in pair] + [side // 2]
     for n, d in enumerate(a_turns):
@@ -264,14 +278,13 @@
             copy(b_ref.at[0, other, i], b_ref.at[0, other, i], s2b.at[d], r2b.at[i], r, sib).wait_recv()
             spread_b(i, d)
 
-    go(a_ref.at[0, x], a_ref.at[1, x], sfa.at[0], rfa.at[x], r, sib)
+    go(a_ref.at[0, x], a_ref.at[1, x], sfa.at[0, 0], rfa.at[x, 0], r, sib)
     go(b_ref.at[0, other], b_ref.at[1, other], sfb.at[0], rfb.at[other], r, sib)
 
-    def pass_a(d):
+    def pass_a(d, j):
         i = turn(x, d, x_side)
-        for j in range(side):
-            copy(a_ref.at[0, i, j], a_ref.at[0, i, j], s3a.at[0, d], r3a.at[i, j], r, sib).wait_recv()
-        go(a_ref.at[0, i], a_ref.at[1, i], sfa.at[d], rfa.at[i], r, sib)
+        copy(a_ref.at[0, i, j], a_ref.at[0, i, j], s3a.at[0, d], r3a.at[i, j], r, sib).wait_recv()
+        go(a_ref.at[0, i, j], a_ref.at[1, i, j], sfa.at[d, j], rfa.at[i, j], r, sib)
 
     def pass_b(d):
         i = turn(other, d, side)
@@ -279,16 +292,21 @@
             copy(b_ref.at[0, i, j], b_ref.at[0, i, j], s3b.at[0, d], r3b.at[i, j], r, sib).wait_recv()
         go(b_ref.at[0, i], b_ref.at[1, i], sfb.at[d], rfb.at[i], r, sib)
 
-    for d in a_turns[:4]:
-        pass_b(d)
-    for d in b_turns:
-        pass_a(d)
+    for n, e in enumerate([0] + a_turns):
+        j = turn(other, e, side)
+        for d in b_turns:
+            pass_a(d, j)
+        if n >= side - 4:
+            pass_b(a_turns[n - side + 4])
     for d in a_turns[4:]:
         pass_b(d)
     for i in range(side):
         copy(b_ref.at[0, i], b_ref.at[1, i], sfb.at[i], rfb.at[i], r, sib).wait_recv()
-    for i in range(x_side):
-        copy(a_ref.at[0, i], a_ref.at[1, i], sfa.at[i], rfa.at[i], r, sib).wait_recv()
+    copy(a_ref.at[0, x], a_ref.at[1, x], sfa.at[0, 0], rfa.at[x, 0], r, sib).wait_recv()
+    for d in range(1, x_side):
+        i = turn(x, d, x_side)
+        for j in range(side):
+            copy(a_ref.at[0, i, j], a_ref.at[1, i, j], sfa.at[d, j], rfa.at[i, j], r, sib).wait_recv()
     copy(eo_ref, eo_ref, se, re, r, sib).wait_recv()
     for one in sends:
         one.wait_send()
@@ -301,7 +319,7 @@
     group = side * 2 * CAP
     cols, rank = emb.shape[1], fac.shape[1]
     dma = pltpu.SemaphoreType.DMA
-    counts = [side, side, side, side, x_side, x_side, (side, x_side), (x_side, side), (x_side, side), (side, x_side), x_side, x_side, side, side]
+    counts = [side, side, side, side, x_side, x_side, (side, x_side), (x_side, side), (x_side, side), (side, x_side), (x_side, side), (x_side, side), side, side]
     return pl.pallas_call(
         functools.partial(gather, sides),
         out_shape=(
@@ -315,7 +333,7 @@
             pltpu.VMEM(emb.shape, BF16),
             pltpu.VMEM(fac.shape, F32),
             pltpu.VMEM(piv.shape, jnp.int32),
-            pltpu.VMEM((side, SUB, cols + rank), F32),
+            pltpu.VMEM((side, GROUPS * group // side, 2 * TILE), BF16),
         ]
         + [dma(n if isinstance(n, tuple) else (n,)) for n in counts]
         + [dma] * 5,

time: 55.7 us -> 55.4 us (level)
  no operation moved by 1% of the time
where the time goes in v5:
time: 55.4 us; the launch traced here: 55.2 us
  Pallas kernels  54.4 us (98%)
  between operations  0.8 us (1%)
    pallas_call x1, Pallas kernels, gather_call(): pl.pallas_call(functools.partial(gather, sides), out_shape=(jax.ShapeDtyp...  37 us
    pallas_call x1, Pallas kernels, extend_call(): pl.pallas_call(functools.partial(extend, sides), out_shape=(jax.ShapeDtyp...  17.4 us

profile of v5, /device:TPU:1, one launch (start us, length us, event | category | flops | bytes accessed | tf_op | source)
XLA Modules:
  0.0 55.2 jit_solution(16532503355751671984)
XLA Ops:
  0.6 37.0 %gather_pivots.1 = (bf16[2,4,8,32,384]{4,3,2,1,0:T(8,128)(2,1)S(1)}, s16[2,8,4,32,256]{4,3,2,1,0:T(8,128)(2,1)S(1)}, bf16[384,384]{1,0:T(8,128)(2,1)S(1)}) custom-call(bf16[768,384]{1,0:T(8,128)(2,1)} %emb_any.3, f32[384,256]{1,0:T(8,128)} %fo_any.1, s32[2,256]{1,0:T(2,128)} %piv_any.3), custom_call_target="tpu_custom_call" | custom-call | tf_op jit(solution)/shard_map/gather_pivots/pallas_call | solution.py:323
  37.7 17.4 %extend.1 = (f32[2,384,256]{2,1,0:T(8,128)}, f32[384]{0:T(512)}) custom-call(s32[2,256]{1,0:T(2,128)} %piv_any.3, bf16[2,4,8,32,384]{4,3,2,1,0:T(8,128)(2,1)S(1)} %get-tuple-element.5.a_ref, s16[2,8,4,32,256]{4,3,2,1,0:T(8,128)(2,1)S(1)} %get-tuple-element.6.b_ref, bf16[768,384]{1,0:T(8,128)(2,1)} %emb_any.3, bf16[384,384]{1,0:T(8,128)(2,1)S(1)} %get-tuple-element.7.es, ...), custom_call_target="tpu_custom_call" | custom-call | tf_op jit(solution)/shard_map/extend/pallas_call | solution.py:513
